TPU v7x, 256 devices: a whole 4x4x8 slice. The times are simulated.
256 devices in a mesh: seq: 16 (over x_hi, z), tp: 8 (over x_lo, y), role: 2 (over core).
Axes of the slice: x: 4 (x_hi: 2, x_lo: 2; x = x_hi * 2 + x_lo), y: 4, z: 8, core: 2. Of those that a mesh axis runs over, the one named last changes fastest.
Arguments:
- prompt_length: int32 [2], P('role'), may hold values from 3073 to 4096, as said below
- owner_map: int32 [8], replicated, may hold values from 0 to 7, as said below
- queries: bfloat16 [2, 4096, 8192], P('role', 'seq', 'tp'), may hold values from -6 to 6
- key_rows: bfloat16 [2, 4096, 1024], P('role', 'seq', 'tp'), may hold values from -6 to 6
- value_matrix: bfloat16 [2, 4096, 1024], P('role', 'seq', 'tp'), may hold values from -6 to 6
- ssm_input: bfloat16 [2, 4096, 16384], P('role', 'seq', 'tp'), may hold values from -6 to 6
- gate_input: bfloat16 [2, 4096, 16384], P('role', 'seq', 'tp'), may hold values from -6 to 6
- step_sizes: bfloat16 [2, 4096, 256], P('role', 'seq', 'tp'), may hold values from 0.049804688 to 0.19921875
- decay_rate: float32 [256], P('tp'), may hold values from 0 to 1
- skip_gain: float32 [256], P('tp'), may hold values from 0.5 to 1.5
- write_proj: bfloat16 [2, 4096, 2048], P('role', 'seq', 'tp'), may hold values from -0.59765625 to 0.59765625
- read_proj: bfloat16 [2, 4096, 2048], P('role', 'seq', 'tp'), may hold values from -0.59765625 to 0.59765625
- norm_gain: float32 [16384], P('tp'), may hold values from 0.1 to 1.9
Outputs:
- mamba_out: bfloat16 [2, 4096, 16384], P('role', 'seq', 'tp')
- attn_out: bfloat16 [2, 4096, 8192], P('role', 'seq', 'tp')
- decode_state: float32 [2, 256, 64, 256], P('role', ('tp', 'seq'))
- decode_kv: bfloat16 [2, 2, 4096, 1024], P('role', None, 'seq', 'tp')
Inputs may be any that keep to these rules, and one draw needn't show every extreme that they name: `prompt_length`: one of the two requests fills all 4096 positions. owner_map[b] = b XOR k for one k from 1 to 7.
All inputs are finite; a program needn't handle non-finite values.
Results may differ from a plain program's by a relative error of at most 0.008.
Values may be sent and summed in bfloat16 or wider, within the bound.
A program may use at most 128 MiB of HBM per device.

v0:
```python
import math

import jax
import jax.numpy as jnp
from jax import lax
from jax.sharding import PartitionSpec as P

MH = 256
P_SIZE = 64
N = 256
GROUPS = 8
QUERY_HEADS = 64
KEY_VALUE_HEADS = 8
HEAD_WIDTH = 128
SPAN = 128


def from_partner(block, axis, apart):
    count = lax.axis_size(axis)
    route = []
    for low in range(count):
        high = low | 1 << apart
        if high != low and high < count:
            route += [(low, high), (high, low)]
    return lax.ppermute(block, axis, route)


def span_core(input_matrix, step_heads, head_rates, write_rows, read_rows, start_state):
    running = jnp.cumsum(-step_heads * head_rates[..., None], axis=-1)
    span_rows = input_matrix.shape[0]
    causal = jnp.arange(span_rows)[:, None] >= jnp.arange(span_rows)[None, :]
    spread = running[..., :, None] - running[..., None, :]
    damping = jnp.where(causal, jnp.exp(jnp.where(causal, spread, 0.0)), 0.0)
    intersection = jnp.einsum(
        "tgn,sgn->gts", read_rows, write_rows, preferred_element_type=jnp.float32
    )
    mixer_kind = (intersection[:, None] * damping * step_heads[..., None, :]).astype(jnp.bfloat16)
    inner_portion = jnp.einsum(
        "wuhy,ywue->hwue", mixer_kind, input_matrix, preferred_element_type=jnp.float32
    )
    carried = jnp.einsum(
        "tgn,grpn->tgrp",
        read_rows,
        start_state.astype(jnp.bfloat16),
        preferred_element_type=jnp.float32,
    )
    carried = carried * jnp.moveaxis(jnp.exp(running), -1, 0)[..., None]
    tail_weight = jnp.exp(running[..., -1:] - running) * step_heads
    weighted = (
        input_matrix.astype(jnp.float32) * jnp.moveaxis(tail_weight, -1, 0)[..., None]
    ).astype(jnp.bfloat16)
    fresh_part = jnp.einsum(
        "sgrp,sgn->grpn", weighted, write_rows, preferred_element_type=jnp.float32
    )
    updated = start_state * jnp.exp(running[..., -1])[..., None, None] + fresh_part
    return (inner_portion + carried, updated)


def scan_spans(input_matrix, step_heads, head_rates, write_rows, read_rows, start_state):
    row_total = input_matrix.shape[0]
    span_count = row_total // SPAN
    groups_here = step_heads.shape[0]
    heads_here = step_heads.shape[1]
    input_spans = input_matrix.reshape((span_count, SPAN) + input_matrix.shape[1:])
    step_spans = jnp.moveaxis(step_heads.reshape(groups_here, heads_here, span_count, SPAN), 2, 0)
    write_spans = write_rows.reshape((span_count, SPAN) + write_rows.shape[1:])
    read_spans = read_rows.reshape((span_count, SPAN) + read_rows.shape[1:])

    def advance(carried_state, pieces):
        mixed_rows, next_state = span_core(
            pieces[0], pieces[1], head_rates, pieces[2], pieces[3], carried_state
        )
        return (next_state, mixed_rows)

    final_state, mixed_spans = lax.scan(
        advance, start_state, (input_spans, step_spans, write_spans, read_spans)
    )
    return (mixed_spans.reshape((row_total,) + mixed_spans.shape[2:]), final_state)


def on_device(
    prompt_length,
    owner_map,
    queries,
    key_rows,
    value_matrix,
    ssm_input,
    gate_input,
    step_sizes,
    decay_rate,
    skip_gain,
    write_proj,
    read_proj,
    norm_gain,
):
    seq_count = lax.axis_size("seq")
    tp_count = lax.axis_size("tp")
    seq_rank = lax.axis_index("seq")
    tok_rows = ssm_input.shape[1]
    length = prompt_length[0]
    positions = seq_rank * tok_rows + jnp.arange(tok_rows, dtype=jnp.int32)
    live_rows = positions < length
    local_kv = KEY_VALUE_HEADS // tp_count
    local_bits = local_kv.bit_length() - 1
    whole_key = owner_map[0]
    route_key = whole_key >> local_bits
    route_levels = tp_count.bit_length() - 1
    kv_local = jnp.stack([key_rows[0], value_matrix[0]])
    kv_local = jnp.where(live_rows[None, :, None], kv_local, jnp.zeros((), jnp.bfloat16))
    moved_key_value = kv_local
    for route_level in range(route_levels + 1):
        partner = from_partner(moved_key_value, ("tp", "role"), route_level)
        if route_level == 0:
            moved_key_value = partner
        else:
            moved_key_value = jnp.where(
                route_key >> route_level - 1 & 1 == 1, partner, moved_key_value
            )
    decode_kv = moved_key_value[None]
    kv_heads = key_rows.shape[2] // HEAD_WIDTH
    heads_per_group = QUERY_HEADS // KEY_VALUE_HEADS
    heads_of_query = queries[0].reshape(tok_rows, kv_heads, heads_per_group, HEAD_WIDTH)
    start_top = jnp.full((kv_heads, heads_per_group, tok_rows), -jnp.inf, jnp.float32)
    start_sum = jnp.zeros((kv_heads, heads_per_group, tok_rows), jnp.float32)
    start_acc = jnp.zeros((kv_heads, heads_per_group, tok_rows, HEAD_WIDTH), jnp.float32)
    keys_piece = lax.all_gather(key_rows[0], "seq", axis=0, tiled=True)
    values_piece = lax.all_gather(value_matrix[0], "seq", axis=0, tiled=True)
    piece_rows = keys_piece.shape[0]
    block_rows = math.gcd(piece_rows, 512)

    def visit_block(block_index, inner_state):
        row_top, denominator, accum = inner_state
        offset = block_index * block_rows
        key_block = lax.dynamic_slice_in_dim(keys_piece, offset, block_rows, 0).reshape(
            block_rows, kv_heads, HEAD_WIDTH
        )
        value_block = lax.dynamic_slice_in_dim(values_piece, offset, block_rows, 0).reshape(
            block_rows, kv_heads, HEAD_WIDTH
        )
        scores = jnp.einsum(
            "tkrd,skd->krts", heads_of_query, key_block, preferred_element_type=jnp.float32
        ) * HEAD_WIDTH ** (-0.5)
        key_pos = offset + jnp.arange(block_rows, dtype=jnp.int32)
        allowed = key_pos[None, :] <= positions[:, None]
        scores = jnp.where(allowed, scores, -jnp.inf)
        new_top = jnp.maximum(row_top, jnp.max(scores, axis=-1))
        stable_top = jnp.where(jnp.isfinite(new_top), new_top, 0.0)
        weights = jnp.exp(scores - stable_top[..., None])
        rescale = jnp.exp(row_top - stable_top)
        denominator = denominator * rescale + jnp.sum(weights, axis=-1)
        accum = accum * rescale[..., None] + jnp.einsum(
            "krts,skd->krtd",
            weights.astype(jnp.bfloat16),
            value_block,
            preferred_element_type=jnp.float32,
        )
        return (new_top, denominator, accum)

    final_top, final_sum, final_acc = lax.fori_loop(
        0, piece_rows // block_rows, visit_block, (start_top, start_sum, start_acc)
    )
    attended = jnp.moveaxis(final_acc / final_sum[..., None], 2, 0).reshape(
        tok_rows, kv_heads * heads_per_group * HEAD_WIDTH
    )
    attn_out = jnp.where(live_rows[:, None], attended, 0.0).astype(jnp.bfloat16)[None]
    local_heads = step_sizes.shape[2]
    local_groups = write_proj.shape[2] // N
    heads_group = MH // GROUPS
    masked_steps = jnp.where(live_rows[:, None], step_sizes[0], jnp.zeros((), jnp.bfloat16))
    head_inputs, head_steps = (
        lax.all_to_all(ssm_input[0], "seq", split_axis=1, concat_axis=0, tiled=True),
        lax.all_to_all(masked_steps, "seq", split_axis=1, concat_axis=0, tiled=True),
    )
    all_writes, all_reads = (
        lax.all_gather(write_proj[0], "seq", axis=0, tiled=True),
        lax.all_gather(read_proj[0], "seq", axis=0, tiled=True),
    )
    slice_heads = local_heads // seq_count
    first_head = seq_rank * slice_heads
    my_writes = all_writes[:, None, :]
    my_reads = all_reads[:, None, :]
    my_rates = lax.dynamic_slice_in_dim(decay_rate, first_head, slice_heads, 0)[None]
    my_skips = lax.dynamic_slice_in_dim(skip_gain, first_head, slice_heads, 0)
    row_total = head_inputs.shape[0]
    shaped = head_inputs.reshape(row_total, 1, slice_heads, P_SIZE)
    step_heads = head_steps.astype(jnp.float32).T.reshape(1, slice_heads, row_total)
    zero_state = jnp.zeros((1, slice_heads, P_SIZE, N), jnp.float32)
    mixed_rows, final_state = scan_spans(
        shaped, step_heads, my_rates, my_writes, my_reads, zero_state
    )
    with_skip = mixed_rows + my_skips[None, None, :, None] * shaped.astype(jnp.float32)
    mixed_bf = with_skip.astype(jnp.bfloat16).reshape(row_total, slice_heads * P_SIZE)
    ssm_tokens = lax.all_to_all(mixed_bf, "seq", split_axis=0, concat_axis=1, tiled=True)
    handed = final_state.reshape(slice_heads, P_SIZE, N)
    gated = ssm_tokens.astype(jnp.float32) * jax.nn.silu(gate_input[0].astype(jnp.float32))
    grouped = gated.reshape(tok_rows, local_groups, heads_group * P_SIZE)
    normed = grouped * lax.rsqrt(jnp.mean(grouped * grouped, axis=-1, keepdims=True) + 1e-05)
    mamba_rows = normed.reshape(tok_rows, local_heads * P_SIZE) * norm_gain[None, :]
    mamba_out = jnp.where(live_rows[:, None], mamba_rows, 0.0).astype(jnp.bfloat16)[None]
    moved_state = handed
    for route_level in range(route_levels + 1):
        partner = from_partner(
            moved_state.astype(jnp.bfloat16), ("tp", "role"), route_level
        ).astype(moved_state.dtype)
        if route_level == 0:
            moved_state = partner
        else:
            moved_state = jnp.where(route_key >> route_level - 1 & 1 == 1, partner, moved_state)
    decode_state = moved_state[None]
    return (mamba_out, attn_out, decode_state, decode_kv)


def solution(mesh):
    in_specs = (
        P("role"),
        P(),
        P("role", "seq", "tp"),
        P("role", "seq", "tp"),
        P("role", "seq", "tp"),
        P("role", "seq", "tp"),
        P("role", "seq", "tp"),
        P("role", "seq", "tp"),
        P("tp"),
        P("tp"),
        P("role", "seq", "tp"),
        P("role", "seq", "tp"),
        P("tp"),
    )
    out_specs = (
        P("role", "seq", "tp"),
        P("role", "seq", "tp"),
        P("role", ("tp", "seq"), None, None),
        P("role", None, "seq", "tp"),
    )
    return jax.shard_map(
        on_device, mesh=mesh, in_specs=in_specs, out_specs=out_specs, check_vma=False
    )
```

profile of v0, /device:TPU:6, one launch (start us, length us, event | category | flops | bytes accessed | tf_op | source)
XLA Modules:
  0.0 548.1 jit_solution(8543084706583808395)
XLA Ops:
  11.4 11.4 %all-to-all-start = ((bf16[256,16,2]{0,2,1:T(2,128)(2,1)}), bf16[256,16,2]{0,2,1:T(2,128)(2,1)S(1)}, u32[]{:S(2)}, u32[]{:S(2)}) async-start(bf16[256,16,2]{0,2,1:T(2,128)(2,1)} %broadcast_select_fusion.2), calls=%async_computation | async-start | bytes 32768 | tf_op jit(solution)/shard_map/all_to_all | solution.py:172
  25.2 4.8 all-to-all-done
  30.0 6.4 %all-to-all-start.1 = ((bf16[256,16,128]{0,2,1:T(8,128)(2,1)}), bf16[256,16,128]{0,2,1:T(8,128)(2,1)S(1)}, u32[]{:S(2)}, u32[]{:S(2)}) async-start(bf16[256,16,128]{0,2,1:T(8,128)(2,1)} %bitcast.5), calls=%async_computation.1 | async-start | bytes 2097152 | tf_op jit(solution)/shard_map/all_to_all | solution.py:171
  39.7 3.9 collective-permute-done.5
  57.2 6.7 %all-to-all-done.1 = bf16[256,16,128]{0,2,1:T(8,128)(2,1)S(1)} async-done(((bf16[256,16,128]{0,2,1:T(8,128)(2,1)}), bf16[256,16,128]{0,2,1:T(8,128)(2,1)S(1)}, u32[]{:S(2)}, u32[]{:S(2)}) %all-to-all-start.1) | async-done | bytes 1048608 | tf_op jit(solution)/shard_map/all_to_all | solution.py:171
  70.3 34.4 %all-gather.9.cloned.1.call-done = bf16[1,4096,256]{2,1,0:T(8,128)(2,1)} async-done(((bf16[1,256,256]{2,1,0:T(8,128)(2,1)}), bf16[1,4096,256]{2,1,0:T(8,128)(2,1)}) %all-gather.9.cloned.1.call-update) | async-done | bytes 2097168 | tf_op jit(solution)/shard_map/all_gather | solution.py:175
  104.7 84.8 %all-gather.11.cloned.1.call-done = bf16[1,4096,256]{2,1,0:T(8,128)(2,1)} async-done(((bf16[1,256,256]{2,1,0:T(8,128)(2,1)}), bf16[1,4096,256]{2,1,0:T(8,128)(2,1)}) %all-gather.11.cloned.1.call-update) | async-done | bytes 2097168 | tf_op jit(solution)/shard_map/all_gather | solution.py:176
  189.4 244.2 %while.31 = (s32[]{:T(128)}, f32[1,2,64,256]{3,2,1,0:T(8,128)S(1)}, f32[32,128,1,2,64]{1,0,4,3,2:T(8,128)}, f32[32,1,2,128]{3,0,2,1:T(8,128)S(1)}, f32[2]{0:T(12...) while((s32[]{:T(128)}, f32[1,2,64,256]{3,2,1,0:T(8,128)S(1)}, ...), condition=%wide.region_2.3_spmd.clone, body=%wide.region_0.2_spmd.clone.sunk | while | flops 29819652 | bytes 1231036 | solution.py:75
  436.6 3.8 fusion.67
  440.4 7.2 %all-to-all-start.2 = ((bf16[16,256,128]{1,2,0:T(8,128)(2,1)}), bf16[16,256,128]{1,2,0:T(8,128)(2,1)S(1)}, u32[]{:S(2)}, u32[]{:S(2)}) async-start(bf16[16,256,128]{1,2,0:T(8,128)(2,1)} %fusion.67), calls=%async_computation.2 | async-start | bytes 2097152 | tf_op jit(solution)/shard_map/all_to_all | solution.py:193
  449.4 77.6 %while.32 = (s32[]{:T(128)}, f32[1,8,256]{2,1,0:T(8,128)S(1)}, f32[1,8,256]{2,1,0:T(8,128)S(1)}, f32[1,8,256,128]{3,2,1,0:T(8,128)}, bf16[4096,128]{1,0:T(8,128)...) while((s32[]{:T(128)}, f32[1,8,256]{2,1,0:T(8,128)S(1)}, ...), condition=%wide.region_7.8_spmd.clone, body=%wide.region_4.7_spmd.clone.sunk | while | flops 549348096 | bytes 32921816 | solution.py:159
  453.2 4.7 fusion.103
  462.6 5.0 fusion.103
  468.7 3.6 fusion.99
  472.3 5.0 fusion.103
  478.4 3.6 fusion.99
  482.1 5.0 fusion.103
  488.2 3.6 fusion.99
  491.8 5.0 fusion.103
  497.9 3.6 fusion.99
  501.6 5.0 fusion.103
  507.7 3.6 fusion.99
  511.3 5.0 fusion.103
  521.0 5.0 fusion.103
  (556 shorter events, 309.1 us)
Async XLA Ops:
  7.2 97.5 %all-gather.9.cloned.1.call-start = ((), (), s32[]{:S(2)}) async-start(), calls=%async_computation.3 | async-start | bytes 2228224 | tf_op jit(solution)/shard_map/all_gather | solution.py:175
  7.9 181.5 %all-gather.11.cloned.1.call-start = ((), (), s32[]{:S(2)}) async-start(), calls=%async_computation.4 | async-start | bytes 2228224 | tf_op jit(solution)/shard_map/all_gather | solution.py:176
  8.6 440.7 %all-gather.13.cloned.1.call-start = ((), (), s32[]{:S(2)}) async-start(), calls=%async_computation.5 | async-start | bytes 1114112 | tf_op jit(solution)/shard_map/all_gather | solution.py:126
  10.8 25.7 %copy-start.7 = (pred[256]{0:T(512)(128)(4,1)}, pred[256]{0:T(512)(128)(4,1)S(1)}, u32[]{:S(2)}) copy-start(pred[256]{0:T(512)(128)(4,1)S(1)} %add_compare_fusion) | copy-start | bytes 772
  11.4 18.6 %all-to-all-start = ((bf16[256,16,2]{0,2,1:T(2,128)(2,1)}), bf16[256,16,2]{0,2,1:T(2,128)(2,1)S(1)}, u32[]{:S(2)}, u32[]{:S(2)}) async-start(bf16[256,16,2]{0,2,1:T(2,128)(2,1)} %broadcast_select_fusion.2), calls=%async_computation | async-start | bytes 32768 | tf_op jit(solution)/shard_map/all_to_all | solution.py:172
  22.9 13.6 %copy-start.2 = (bf16[1,256,128]{2,1,0:T(8,128)(2,1)S(1)}, bf16[1,256,128]{2,1,0:T(8,128)(2,1)}, u32[]{:S(2)}) copy-start(bf16[1,256,128]{2,1,0:T(8,128)(2,1)} %param.20) | copy-start | bytes 196612
  22.9 13.7 %copy-start.3 = (bf16[1,256,128]{2,1,0:T(8,128)(2,1)S(1)}, bf16[1,256,128]{2,1,0:T(8,128)(2,1)}, u32[]{:S(2)}) copy-start(bf16[1,256,128]{2,1,0:T(8,128)(2,1)} %param.21) | copy-start | bytes 196612
  22.9 16.8 %copy-start.10 = (s32[8]{0:T(128)S(1)}, s32[8]{0:T(128)}, u32[]{:S(2)}) copy-start(s32[8]{0:T(128)} %param.18) | copy-start | bytes 100
  25.2 26.0 %copy-start.11 = (f32[32]{0:T(128)S(1)}, f32[32]{0:T(128)}, u32[]{:S(2)}) copy-start(f32[32]{0:T(128)} %param.25) | copy-start | bytes 388
  25.2 26.6 %copy-start.12 = (f32[32]{0:T(128)S(1)}, f32[32]{0:T(128)}, u32[]{:S(2)}) copy-start(f32[32]{0:T(128)} %param.26) | copy-start | bytes 388
  30.0 22.0 %copy-start.4 = (bf16[256,16,2]{0,2,1:T(2,128)(2,1)}, bf16[256,16,2]{0,2,1:T(2,128)(2,1)S(1)}, u32[]{:S(2)}) copy-start(bf16[256,16,2]{0,2,1:T(2,128)(2,1)S(1)} %all-to-all-done) | copy-start | bytes 49156
  30.0 33.9 %all-to-all-start.1 = ((bf16[256,16,128]{0,2,1:T(8,128)(2,1)}), bf16[256,16,128]{0,2,1:T(8,128)(2,1)S(1)}, u32[]{:S(2)}, u32[]{:S(2)}) async-start(bf16[256,16,128]{0,2,1:T(8,128)(2,1)} %bitcast.5), calls=%async_computation.1 | async-start | bytes 2097152 | tf_op jit(solution)/shard_map/all_to_all | solution.py:171
  36.4 17.7 %copy-start.1 = (bf16[1,256,1024]{2,1,0:T(8,128)(2,1)S(1)}, bf16[1,256,1024]{2,1,0:T(8,128)(2,1)}, u32[]{:S(2)}) copy-start(bf16[1,256,1024]{2,1,0:T(8,128)(2,1)} %param.19) | copy-start | bytes 1572868
  36.5 412.9 %all-gather.15.cloned.1.call-start = ((), (), s32[]{:S(2)}) async-start(), calls=%async_computation.6 | async-start | bytes 1114112 | tf_op jit(solution)/shard_map/all_gather | solution.py:127
  36.6 1.4 collective-permute-start.4
  38.1 5.6 %collective-permute-start.5 = (bf16[2,256,128]{2,1,0:T(8,128)(2,1)S(1)}, bf16[2,256,128]{2,1,0:T(8,128)(2,1)S(1)}, u32[]{:S(2)}, u32[]{:S(2)}) collective-permute-start(bf16[2,256,128]{2,1,0:T(8,128)(2,1)S(1)} %collective-permute-done.4), channel_id=1, source_target_pairs={{0,2},{2,0},{1,3},{3,1},{4,6},{6,4},{5,7},{7,5},{8,10},{10,8},{9,1... | collective-permute-start | bytes 393224 | tf_op jit(solution)/shard_map/ppermute | solution.py:25
  43.6 6.6 %collective-permute-start.6 = (bf16[2,256,128]{2,1,0:T(8,128)(2,1)S(1)}, bf16[2,256,128]{2,1,0:T(8,128)(2,1)S(1)}, u32[]{:S(2)}, u32[]{:S(2)}) collective-permute-start(bf16[2,256,128]{2,1,0:T(8,128)(2,1)S(1)} %broadcast_select_fusion), channel_id=1, source_target_pairs={{0,4},{4,0},{1,5},{5,1},{2,6},{6,2},{3,7},{7,3},{8,12},{12,8},{9,1... | collective-permute-start | bytes 393224 | tf_op jit(solution)/shard_map/ppermute | solution.py:25
  50.2 6.3 %collective-permute-start.7 = (bf16[2,256,128]{2,1,0:T(8,128)(2,1)S(1)}, bf16[2,256,128]{2,1,0:T(8,128)(2,1)S(1)}, u32[]{:S(2)}, u32[]{:S(2)}) collective-permute-start(bf16[2,256,128]{2,1,0:T(8,128)(2,1)S(1)} %broadcast_select_fusion.1), channel_id=1, source_target_pairs={{0,8},{8,0},{1,9},{9,1},{2,10},{10,2},{3,11},{11,3},{4,12},{12,4},... | collective-permute-start | bytes 393224 | tf_op jit(solution)/shard_map/ppermute | solution.py:25
  65.4 124.0 %copy-start.5 = (f32[2]{0:T(128)S(1)}, f32[2]{0:T(128)}, u32[]{:S(2)}) copy-start(f32[2]{0:T(128)} %dynamic_slice.35) | copy-start | bytes 28
  433.6 14.0 %collective-permute-start = (bf16[2,64,256]{2,1,0:T(8,128)(2,1)S(1)}, bf16[2,64,256]{2,1,0:T(8,128)(2,1)S(1)}, u32[]{:S(2)}, u32[]{:S(2)}) collective-permute-start(bf16[2,64,256]{2,1,0:T(8,128)(2,1)S(1)} %convert_bitcast_fusion), channel_id=1, source_target_pairs={{0,1},{1,0},{2,3},{3,2},{4,5},{5,4},{6,7},{7,6},{8,9},{9,8},{10,11... | collective-permute-start | bytes 196616 | tf_op jit(solution)/shard_map/ppermute | solution.py:25
  440.4 97.5 %all-to-all-start.2 = ((bf16[16,256,128]{1,2,0:T(8,128)(2,1)}), bf16[16,256,128]{1,2,0:T(8,128)(2,1)S(1)}, u32[]{:S(2)}, u32[]{:S(2)}) async-start(bf16[16,256,128]{1,2,0:T(8,128)(2,1)} %fusion.67), calls=%async_computation.2 | async-start | bytes 2097152 | tf_op jit(solution)/shard_map/all_to_all | solution.py:193
  447.6 79.4 %collective-permute-start.1 = (bf16[2,64,256]{2,1,0:T(8,128)(2,1)S(1)}, bf16[2,64,256]{2,1,0:T(8,128)(2,1)S(1)}, u32[]{:S(2)}, u32[]{:S(2)}) collective-permute-start(bf16[2,64,256]{2,1,0:T(8,128)(2,1)S(1)} %collective-permute-done), channel_id=1, source_target_pairs={{0,2},{2,0},{1,3},{3,1},{4,6},{6,4},{5,7},{7,5},{8,10},{10,8},{9,1... | collective-permute-start | bytes 196616 | tf_op jit(solution)/shard_map/ppermute | solution.py:25
  527.0 5.9 %collective-permute-start.2 = (bf16[2,64,256]{2,1,0:T(8,128)(2,1)S(1)}, bf16[2,64,256]{2,1,0:T(8,128)(2,1)S(1)}, u32[]{:S(2)}, u32[]{:S(2)}) collective-permute-start(bf16[2,64,256]{2,1,0:T(8,128)(2,1)S(1)} %fusion.68), channel_id=1, source_target_pairs={{0,4},{4,0},{1,5},{5,1},{2,6},{6,2},{3,7},{7,3},{8,12},{12,8},{9,1... | collective-permute-start | bytes 196616 | tf_op jit(solution)/shard_map/ppermute | solution.py:25
  532.9 4.4 collective-permute-start.3
  (11 other events, 49.4 us)
Sparse Core Ops, SparseCore 0:
  10.6 94.0 all-gather.8
  107.3 82.1 all-gather.10
  192.0 75.4 all-gather.12
  270.0 75.6 all-gather.14
where the time goes:
time: 556 us; the launch traced here: 548 us
  matrix products  197 us (35%)
  waiting for transfers between devices  147 us (26%)
  local copies, waits for them, and re-layouts  116 us (21%)
  starting transfers between devices  35.8 us (6%)
  other arithmetic  34.8 us (6%)
  between operations  14.8 us (3%)
    dynamic_update_slice x32, local copies, waits for them, and re-layouts, scan_spans(): lax.scan(advance, start_state, (input_spans, step_spans, write_spans, rea...  91.3 us
    all_gather x1, waiting for transfers between devices, on_device(): lax.all_gather(read_proj[0], 'seq', axis=0, tiled=True)  84.8 us
    dot_general x8, matrix products, visit_block(): jnp.einsum('krts,skd->krtd', weights.astype(jnp.bfloat16), value_block, p...  39.7 us
    all_gather x1, waiting for transfers between devices, on_device(): lax.all_gather(write_proj[0], 'seq', axis=0, tiled=True)  34.4 us
    dot_general x32, matrix products, span_core(): jnp.einsum('sgrp,sgn->grpn', weighted, write_rows, preferred_element_type...  32.6 us
    dot_general x32, matrix products, span_core(): jnp.einsum('tgn,grpn->tgrp', read_rows, start_state.astype(jnp.bfloat16),...  32.5 us
    dot_general x32, matrix products, span_core(): jnp.einsum('tgn,sgn->gts', read_rows, write_rows, preferred_element_type=...  31.8 us
    dot_general x32, matrix products, span_core(): jnp.einsum('wuhy,ywue->hwue', mixer_kind, input_matrix, preferred_element...  31.7 us
  transfers between devices with their start and end apart: 15, of which 10 were waited for; matrix products, arithmetic and copies ran while one was open for 63% of the time, Pallas kernels for 0%

commit v1 on v0

v1 whole, which is shorter than its diff:
```python
import jax
import jax.numpy as jnp
from jax import lax
from jax.experimental import pallas as pl
from jax.experimental.pallas import tpu as pltpu
from jax.sharding import PartitionSpec as P

MESH = pl.DeviceIdType.MESH
LOG2E = 1.4426950408889634
SCORE = 128**-0.5 * LOG2E
ROWS = 256
LANES = 128
SEQ = 16
RING = 8
HEADS = 8
STATE = 256
MSG = STATE + 16
F32 = jnp.float32
BF16 = jnp.bfloat16


def iota(shape, dim):
    return lax.broadcasted_iota(jnp.int32, shape, dim)


def pair_columns(table, pair):
    turned = pltpu.roll(table, lax.rem(LANES - 2 * pair, LANES), axis=1)
    low = iota(table.shape, 1) < 64
    return jnp.where(low, turned[:, 0:1], turned[:, 1:2])


def kernel(
    len_ref,
    own_ref,
    q_ref,
    k_ref,
    v_ref,
    x_ref,
    g_ref,
    st_ref,
    rate_ref,
    skip_ref,
    b_ref,
    c_ref,
    gain_ref,
    mo_ref,
    ao_ref,
    ds_ref,
    dk_ref,
    kvo,
    kvx,
    tx1,
    rx1,
    tx2,
    rx2,
    hkt,
    hkr,
    hst,
    hsr,
    log_ref,
    w_ref,
    e_ref,
    mt_ref,
    bt_ref,
    gm_ref,
    y_ref,
    el_ref,
    sg_ref,
    top_ref,
    acc_ref,
    state_ref,
    sq_ref,
    s1,
    r1,
    s2,
    r2,
    so,
    ro,
    sx,
    rx,
    sk,
    rk,
    sf,
    rf,
):
    s, t, r = lax.axis_index("seq"), lax.axis_index("tp"), lax.axis_index("role")
    row = s // RING
    z = lax.rem(s, RING)
    across = (lax.rem(s + RING, SEQ), t, r)

    def on_ring(step):
        return (row * RING + lax.rem(z + step + RING, RING), t, r)

    def owner_hop(level):
        if level == 0:
            return (s, t, 1 - r)
        width = 1 << (level - 1)
        return (s, t + width * (1 - 2 * lax.rem(t // width, 2)), r)

    def send(src, dst, ssem, rsem, device):
        return pltpu.make_async_remote_copy(
            src, dst, ssem, rsem, device_id=device, device_id_type=MESH
        )

    barrier = pltpu.get_barrier_semaphore()
    for k in range(1, SEQ):
        pl.semaphore_signal(
            barrier, inc=1, device_id=(lax.rem(s + k, SEQ), t, r), device_id_type=MESH
        )
    for level in range(4):
        pl.semaphore_signal(barrier, inc=1, device_id=owner_hop(level), device_id_type=MESH)

    length = len_ref[0]
    live = s * ROWS + iota((ROWS, LANES), 0) < length
    low = iota((ROWS, LANES), 1) < 64
    kvo[0, 0] = jnp.where(live, k_ref[0].astype(F32), 0.0).astype(BF16)
    kvo[0, 1] = jnp.where(live, v_ref[0].astype(F32), 0.0).astype(BF16)
    pl.semaphore_wait(barrier, SEQ - 1 + 4)

    def ring_copy(src, dst, device):
        return send(kvo.at[src], kvo.at[dst], so.at[dst], ro.at[dst], device)

    def cross_copy(slot):
        return send(kvo.at[slot], kvx.at[slot], sx.at[slot], rx.at[slot], across)

    def kv_hop(level):
        src = kvo.at[0] if level == 0 else hkt.at[level]
        return send(src, hkr.at[level], sk.at[level], rk.at[level], owner_hop(level))

    def state_hop(level):
        return send(
            hst.at[level], hsr.at[level], sf.at[level], rf.at[level], owner_hop(level)
        )

    def local_copy(k, device):
        return send(tx1.at[k], rx1.at[k], s1.at[k], r1.at[k], device)

    def prefix_copy(k, device):
        return send(tx2.at[k], rx2.at[k], s2.at[k], r2.at[k], device)

    ring_copy(0, RING - 1, on_ring(1)).start()
    ring_copy(0, 1, on_ring(-1)).start()

    @pl.when(row == 0)
    def _():
        cross_copy(0).start()

    kv_hop(0).start()

    steps = jnp.concatenate(
        [st_ref[0].astype(F32), jnp.zeros((ROWS, LANES - 32), F32)], axis=1
    )
    rates = jnp.concatenate([rate_ref[...], jnp.zeros((1, LANES - 32), F32)], axis=1)
    steps = jnp.where(live, steps, 0.0)
    causal = iota((ROWS, ROWS), 0) >= iota((ROWS, ROWS), 1)
    logs = jnp.dot(
        causal.astype(F32),
        steps * rates * -LOG2E,
        precision=lax.Precision.HIGHEST,
        preferred_element_type=F32,
    )
    used = steps > 0.0
    less = jnp.where(used, logs - jnp.log(jnp.where(used, steps, 1.0)) * LOG2E, 1e9)
    log_ref[...] = logs
    w_ref[...] = jnp.exp2(logs[ROWS - 1 :, :] - less)
    e_ref[...] = jnp.exp2(logs)
    mt_ref[...] = less.T
    bt_ref[...] = b_ref[0].astype(F32).T.astype(BF16)

    def local_state(k, carry):
        pair = lax.rem(s + k, SEQ)
        cols = pl.ds(pl.multiple_of(pair * LANES, LANES), LANES)
        weight = pair_columns(w_ref[...], pair)
        weighted = (x_ref[0, :, cols].astype(F32) * weight).astype(BF16)
        fresh = jnp.dot(bt_ref[...], weighted, preferred_element_type=F32)
        decay = pair_columns(e_ref[ROWS - 8 :, :], pair)[7:8, :]
        high = decay.astype(BF16).astype(F32)
        middle = (decay - high).astype(BF16).astype(F32)
        rest = decay - high - middle
        which = iota((16, LANES), 0)
        parts = jnp.where(
            which == 0, high, jnp.where(which == 1, middle, jnp.where(which == 2, rest, 0.0))
        )
        tx1[k, :STATE, :] = fresh.astype(BF16)
        tx1[k, STATE:, :] = parts.astype(BF16)

        @pl.when(k == 0)
        def _():
            rx1[0, :STATE, :] = fresh.astype(BF16)
            rx1[0, STATE:, :] = parts.astype(BF16)

        @pl.when(k > 0)
        def _():
            local_copy(k, (pair, t, r)).start()

        return carry

    lax.fori_loop(0, SEQ, local_state, 0)

    gm_ref[...] = jnp.where(
        causal,
        lax.dot_general(
            c_ref[0], b_ref[0], (((1,), (1,)), ((), ())), preferred_element_type=F32
        ),
        0.0,
    )

    def within(pair, carry):
        cols = pl.ds(pl.multiple_of(pair * LANES, LANES), LANES)
        turned = pltpu.roll(log_ref[...], lax.rem(LANES - 2 * pair, LANES), axis=1)
        columns = [jnp.broadcast_to(turned[:, i : i + 1], (ROWS, LANES)) for i in range(2)]
        lines = [mt_ref[pl.ds(2 * pair + i, 1), :] for i in range(2)]
        x = x_ref[0, :, cols].astype(F32)
        halves = [jnp.where(low, x, 0.0).astype(BF16), jnp.where(low, 0.0, x).astype(BF16)]

        def mix(head, down, right):
            rows, over = slice(down, down + 128), slice(right, right + 128)
            spread = columns[head][rows] - lines[head][:, over]
            return (gm_ref[rows, over] * jnp.exp2(spread)).astype(BF16)

        skips = jnp.concatenate([skip_ref[...], jnp.zeros((1, LANES - 32), F32)], axis=1)
        skipped = pair_columns(jnp.broadcast_to(skips, (8, LANES)), pair)[0:1, :] * x
        upper = jnp.dot(
            jnp.concatenate([mix(0, 0, 0), mix(1, 0, 0)], axis=1),
            jnp.concatenate([halves[0][:128], halves[1][:128]], axis=0),
            preferred_element_type=F32,
        )
        lower = jnp.dot(
            jnp.concatenate(
                [mix(0, 128, 0), mix(0, 128, 128), mix(1, 128, 0), mix(1, 128, 128)], axis=1
            ),
            jnp.concatenate(halves, axis=0),
            preferred_element_type=F32,
        )
        y_ref[:128, cols] = upper + skipped[:128]
        y_ref[128:, cols] = lower + skipped[128:]
        el_ref[:, cols] = jnp.exp2(jnp.where(low, columns[0], columns[1]))
        gate = g_ref[0, :, cols].astype(F32)
        sg_ref[:, cols] = gate / (1.0 + jnp.exp(-gate))
        return carry

    def attend(keys, values, diagonal):
        extended = jnp.concatenate([values, jnp.ones((ROWS, LANES), BF16)], axis=1)

        def head(h, carry):
            cols = pl.ds(pl.multiple_of(h * LANES, LANES), LANES)
            scores = lax.dot_general(
                q_ref[0, :, cols], keys, (((1,), (1,)), ((), ())), preferred_element_type=F32
            )
            scores = scores * SCORE
            if diagonal:
                scores = jnp.where(causal, scores, -jnp.inf)
            peak = jnp.max(scores, axis=1, keepdims=True)
            if diagonal:
                top = jnp.broadcast_to(peak, (ROWS, LANES))
            else:
                before = top_ref[h]
                top = jnp.maximum(before, peak)
            weights = jnp.concatenate(
                [jnp.exp2(scores[:, :LANES] - top), jnp.exp2(scores[:, LANES:] - top)], axis=1
            ).astype(BF16)
            part = jnp.dot(weights, extended, preferred_element_type=F32)
            top_ref[h] = top
            if diagonal:
                acc_ref[h] = part
            else:
                scale = jnp.exp2(before - top)
                acc_ref[h] = acc_ref[h] * jnp.concatenate([scale, scale], axis=1) + part
            return carry

        lax.fori_loop(0, HEADS, head, 0)

    attend(kvo[0, 0], kvo[0, 1], True)
    lax.fori_loop(0, 2, within, 0)

    key_xor = own_ref[0]

    def routed(level, arrived, held):
        bit = lax.rem(key_xor // (1 << (level - 1)), 2)
        take = jnp.broadcast_to(bit, arrived.shape) == 1
        return jnp.where(take, arrived.astype(F32), held.astype(F32)).astype(BF16)

    def kv_step(level):
        kv_hop(level).wait_recv()
        for part in range(2):
            moved = hkr[level, part]
            if level > 0:
                moved = routed(level, moved, hkt[level, part])
            if level < 3:
                hkt[level + 1, part] = moved
            else:
                dk_ref[0, part] = moved
        if level < 3:
            kv_hop(level + 1).start()

    def own_row(turn, carry):
        half = (turn + 1) // 2
        slot = jnp.where(lax.rem(turn, 2) == 1, RING - half, half)
        lax.fori_loop(2 * turn, 2 * turn + 2, within, 0)
        for level in range(4):

            @pl.when(turn == 2 * level + 1)
            def _():
                kv_step(level)

        ring_copy(0, slot, on_ring(1)).wait_recv()
        forward = slot >= 4

        @pl.when(jnp.logical_and(slot != 4, slot != 3))
        def _():
            step = jnp.where(forward, 1, -1)
            ring_copy(slot, slot - step, on_ring(step)).start()

        @pl.when(row == 0)
        def _():
            cross_copy(slot).start()

        @pl.when(lax.rem(z + slot, RING) < z)
        def _():
            attend(kvo[slot, 0], kvo[slot, 1], False)

        return carry

    lax.fori_loop(1, RING, own_row, 0)

    state_ref[...] = jnp.zeros((STATE, LANES), F32)

    def scan(i, carry):
        ahead = lax.rem(i - s + SEQ, SEQ)
        now = state_ref[...]
        tx2[ahead] = now.astype(BF16)

        @pl.when(ahead == 0)
        def _():
            rx2[0] = now.astype(BF16)

        @pl.when(ahead > 0)
        def _():
            prefix_copy(ahead, (i, t, r)).start()

        behind = lax.rem(s - i + SEQ, SEQ)

        @pl.when(behind > 0)
        def _():
            local_copy(behind, (i, t, r)).wait_recv()

        decay = jnp.sum(rx1[behind, STATE:, :].astype(F32), axis=0, keepdims=True)
        state_ref[...] = now * decay + rx1[behind, :STATE, :].astype(F32)
        return carry

    lax.fori_loop(0, SEQ, scan, 0)
    hst[0] = state_ref[...].astype(BF16)
    state_hop(0).start()

    def state_step(level):
        state_hop(level).wait_recv()
        moved = hsr[level]
        if level > 0:
            moved = routed(level, moved, hst[level])
        if level < 3:
            hst[level + 1] = moved
            state_hop(level + 1).start()
        else:
            ds_ref[0] = moved.astype(F32).T.reshape(2, 64, STATE)

    def other_row(turn, carry):
        half = (turn + 1) // 2
        slot = jnp.where(lax.rem(turn, 2) == 1, RING - half, half)

        @pl.when(row == 1)
        def _():
            cross_copy(slot).wait_recv()
            attend(kvx[slot, 0], kvx[slot, 1], False)

        for level in range(4):

            @pl.when(turn == 2 * level + 1)
            def _():
                state_step(level)

        return carry

    lax.fori_loop(0, RING, other_row, 0)

    def finish(h, carry):
        cols = pl.ds(pl.multiple_of(h * LANES, LANES), LANES)
        both = acc_ref[h]
        ao_ref[0, :, cols] = jnp.where(live, both[:, :LANES] / both[:, LANES:], 0.0).astype(BF16)
        return carry

    lax.fori_loop(0, HEADS, finish, 0)

    sq_ref[...] = jnp.zeros((ROWS, LANES), F32)

    def outputs(k, carry):
        pair = lax.rem(s - k + SEQ, SEQ)
        cols = pl.ds(pl.multiple_of(pair * LANES, LANES), LANES)

        @pl.when(k > 0)
        def _():
            prefix_copy(k, (pair, t, r)).wait_recv()

        carried = jnp.dot(c_ref[0], rx2[k], preferred_element_type=F32)
        mixed = (y_ref[:, cols] + el_ref[:, cols] * carried).astype(BF16).astype(F32)
        gated = mixed * sg_ref[:, cols]
        y_ref[:, cols] = gated
        sq_ref[...] += gated * gated
        return carry

    lax.fori_loop(0, SEQ, outputs, 0)
    mean = jnp.sum(sq_ref[...], axis=1, keepdims=True) * (1.0 / 2048.0)
    factor = jnp.where(live, lax.rsqrt(mean + 1e-05), 0.0)

    def norm(pair, carry):
        cols = pl.ds(pl.multiple_of(pair * LANES, LANES), LANES)
        mo_ref[0, :, cols] = (y_ref[:, cols] * factor * gain_ref[:, cols]).astype(BF16)
        return carry

    lax.fori_loop(0, SEQ, norm, 0)

    def sent(k, carry):
        local_copy(k, (lax.rem(s + k, SEQ), t, r)).wait_send()
        prefix_copy(k, (lax.rem(s + k, SEQ), t, r)).wait_send()
        return carry

    lax.fori_loop(1, SEQ, sent, 0)
    for slot in range(1, RING):
        ring_copy(0, slot, on_ring(1)).wait_send()

    @pl.when(row == 0)
    def _():
        for slot in range(RING):
            cross_copy(slot).wait_send()

    for level in range(4):
        kv_hop(level).wait_send()
        state_hop(level).wait_send()


def on_device(
    prompt_length,
    owner_map,
    queries,
    key_rows,
    value_matrix,
    ssm_input,
    gate_input,
    step_sizes,
    decay_rate,
    skip_gain,
    write_proj,
    read_proj,
    norm_gain,
):
    smem = pl.BlockSpec(memory_space=pltpu.SMEM)
    vmem = pl.BlockSpec(memory_space=pltpu.VMEM)
    dma = pltpu.SemaphoreType.DMA
    wide = pltpu.VMEM((ROWS, SEQ * LANES), F32)
    square = pltpu.VMEM((ROWS, LANES), F32)
    return pl.pallas_call(
        kernel,
        name="prefill",
        out_shape=(
            jax.ShapeDtypeStruct((1, ROWS, 2048), BF16),
            jax.ShapeDtypeStruct((1, ROWS, 1024), BF16),
            jax.ShapeDtypeStruct((1, 2, 64, STATE), F32),
            jax.ShapeDtypeStruct((1, 2, ROWS, LANES), BF16),
        ),
        in_specs=[smem, smem] + [vmem] * 11,
        out_specs=(vmem,) * 4,
        scratch_shapes=[
            pltpu.VMEM((RING, 2, ROWS, LANES), BF16),
            pltpu.VMEM((RING, 2, ROWS, LANES), BF16),
            pltpu.VMEM((SEQ, MSG, LANES), BF16),
            pltpu.VMEM((SEQ, MSG, LANES), BF16),
            pltpu.VMEM((SEQ, STATE, LANES), BF16),
            pltpu.VMEM((SEQ, STATE, LANES), BF16),
            pltpu.VMEM((4, 2, ROWS, LANES), BF16),
            pltpu.VMEM((4, 2, ROWS, LANES), BF16),
            pltpu.VMEM((4, STATE, LANES), BF16),
            pltpu.VMEM((4, STATE, LANES), BF16),
            square,
            square,
            square,
            pltpu.VMEM((LANES, ROWS), F32),
            pltpu.VMEM((STATE, ROWS), BF16),
            pltpu.VMEM((ROWS, ROWS), F32),
            wide,
            wide,
            wide,
            pltpu.VMEM((HEADS, ROWS, LANES), F32),
            pltpu.VMEM((HEADS, ROWS, 2 * LANES), F32),
            pltpu.VMEM((STATE, LANES), F32),
            square,
            dma((SEQ,)),
            dma((SEQ,)),
            dma((SEQ,)),
            dma((SEQ,)),
            dma((RING,)),
            dma((RING,)),
            dma((RING,)),
            dma((RING,)),
            dma((4,)),
            dma((4,)),
            dma((4,)),
            dma((4,)),
        ],
        compiler_params=pltpu.CompilerParams(
            collective_id=0, has_side_effects=True, vmem_limit_bytes=48 * 2**20
        ),
    )(
        prompt_length,
        owner_map,
        queries,
        key_rows,
        value_matrix,
        ssm_input,
        gate_input,
        step_sizes,
        decay_rate.reshape(1, 32),
        skip_gain.reshape(1, 32),
        write_proj,
        read_proj,
        norm_gain.reshape(1, 2048),
    )


def solution(mesh):
    tokens = P("role", "seq", "tp")
    in_specs = (
        P("role"),
        P(),
        tokens,
        tokens,
        tokens,
        tokens,
        tokens,
        tokens,
        P("tp"),
        P("tp"),
        tokens,
        tokens,
        P("tp"),
    )
    out_specs = (
        tokens,
        tokens,
        P("role", ("tp", "seq"), None, None),
        P("role", None, "seq", "tp"),
    )
    return jax.shard_map(
        on_device, mesh=mesh, in_specs=in_specs, out_specs=out_specs, check_vma=False
    )
```

time: 556 us -> 100 us (0.18)
  the two profiles are of different devices: /device:TPU:6 before, /device:TPU:230 now
where the time goes in v1:
time: 100 us; the launch traced here: 99.8 us
  Pallas kernels  88.3 us (88%)
  local copies, waits for them, and re-layouts  10.1 us (10%)
  between operations  1.41 us (1%)
    pallas_call x1, Pallas kernels, on_device(): pl.pallas_call(kernel, name='prefill', out_shape=(jax.ShapeDtypeStruct((1...  88.3 us
    unnamed x27, local copies, waits for them, and re-layouts  10.1 us

profile of v1, /device:TPU:230, one launch (start us, length us, event | category | flops | bytes accessed | tf_op | source)
XLA Modules:
  0.0 99.8 jit_solution(4217287636105769599)
XLA Ops:
  0.6 0.0 copy-start.5
  1.3 0.0 copy-start.7
  1.3 0.0 copy-start.8
  1.3 0.0 copy-start.9
  1.4 0.0 copy-start.10
  1.4 0.9 copy.17.st_ref
  2.2 0.0 copy-done.5
  2.2 0.0 copy-done.7
  2.2 0.0 copy-done.8
  2.2 0.0 copy-done.9
  2.3 0.0 copy-done.10
  2.3 0.0 copy-start
  2.3 1.2 %copy-done = bf16[1,256,2048]{2,1,0:T(8,128)(2,1)S(1)} copy-done((bf16[1,256,2048]{2,1,0:T(8,128)(2,1)S(1)}, bf16[1,256,2048]{2,1,0:T(8,128)(2,1)}, u32[]{:S(2)}) %copy-start) | copy-done | bytes 1048600
  3.5 0.0 copy-start.1
  3.5 1.2 %copy-done.1 = bf16[1,256,2048]{2,1,0:T(8,128)(2,1)S(1)} copy-done((bf16[1,256,2048]{2,1,0:T(8,128)(2,1)S(1)}, bf16[1,256,2048]{2,1,0:T(8,128)(2,1)}, u32[]{:S(2)}) %copy-start.1) | copy-done | bytes 1048600
  4.7 1.0 %copy-done.2 = bf16[1,256,1024]{2,1,0:T(8,128)(2,1)S(1)} copy-done((bf16[1,256,1024]{2,1,0:T(8,128)(2,1)S(1)}, bf16[1,256,1024]{2,1,0:T(8,128)(2,1)}, u32[]{:S(2)}) %copy-start.2) | copy-done | bytes 524312
  5.8 0.9 copy-done.3
  6.7 0.9 copy-done.4
  7.6 0.8 copy-done.6
  8.4 88.3 %prefill.1 = (bf16[1,256,2048]{2,1,0:T(8,128)(2,1)S(1)}, bf16[1,256,1024]{2,1,0:T(8,128)(2,1)S(1)}, f32[1,2,64,256]{3,2,1,0:T(8,128)S(1)}, bf16[1,2,256,128]{3,2,1,0:T(8,128)(2,1)S(1)}) custom-call(s32[1]{0:T(128)S(6)} %copy.22.len_ref, s32[8]{0:T(128)S(1)} %copy-done.8, bf16[1,256,1024]{2,1,0:T(8,128)(2,1)S(1)} %copy-done.2, ...), custom_call_target="tpu_custom_call" | custom-call | tf_op jit(solution)/shard_map/prefill/pallas_call | solution.py:460
  96.7 1.0 copy.23
  97.7 0.8 copy.24
  98.5 0.7 copy.25
  99.1 0.7 copy.26
  (4 shorter events, 0.0 us)
Async XLA Ops:
  0.6 1.6 %copy-start.5 = (bf16[1,256,128]{2,1,0:T(8,128)(2,1)S(1)}, bf16[1,256,128]{2,1,0:T(8,128)(2,1)}, u32[]{:S(2)}) copy-start(bf16[1,256,128]{2,1,0:T(8,128)(2,1)} %k_ref.1) | copy-start | bytes 196612
  1.3 0.9 copy-start.7
  1.3 0.9 copy-start.8
  1.3 0.9 copy-start.9
  1.4 0.9 copy-start.10
  2.3 1.2 %copy-start = (bf16[1,256,2048]{2,1,0:T(8,128)(2,1)S(1)}, bf16[1,256,2048]{2,1,0:T(8,128)(2,1)}, u32[]{:S(2)}) copy-start(bf16[1,256,2048]{2,1,0:T(8,128)(2,1)} %x_ref.1) | copy-start | bytes 3145732
  3.5 1.2 %copy-start.1 = (bf16[1,256,2048]{2,1,0:T(8,128)(2,1)S(1)}, bf16[1,256,2048]{2,1,0:T(8,128)(2,1)}, u32[]{:S(2)}) copy-start(bf16[1,256,2048]{2,1,0:T(8,128)(2,1)} %g_ref.1) | copy-start | bytes 3145732
  4.7 1.0 %copy-start.2 = (bf16[1,256,1024]{2,1,0:T(8,128)(2,1)S(1)}, bf16[1,256,1024]{2,1,0:T(8,128)(2,1)}, u32[]{:S(2)}) copy-start(bf16[1,256,1024]{2,1,0:T(8,128)(2,1)} %q_ref.1) | copy-start | bytes 1572868
  5.8 0.9 copy-start.3
  6.7 0.9 copy-start.4
  7.6 0.8 copy-start.6

commit v2 on v1

v2 whole, which is shorter than its diff:
```python
import jax
import jax.numpy as jnp
from jax import lax
from jax.experimental import pallas as pl
from jax.experimental.pallas import tpu as pltpu
from jax.sharding import PartitionSpec as P

MESH = pl.DeviceIdType.MESH
LOG2E = 1.4426950408889634
SCORE = 128**-0.5 * LOG2E
ROWS = 256
LANES = 128
SEQ = 16
RING = 8
HEADS = 8
STATE = 256
MSG = STATE + 16
F32 = jnp.float32
BF16 = jnp.bfloat16


def iota(shape, dim):
    return lax.broadcasted_iota(jnp.int32, shape, dim)


def kernel(
    len_ref,
    own_ref,
    q_hbm,
    k_hbm,
    v_hbm,
    x_hbm,
    g_hbm,
    st_ref,
    rate_ref,
    skip_ref,
    b_hbm,
    c_hbm,
    y_ref,
    sq_ref,
    ao_ref,
    ds_ref,
    dk_ref,
    q_ref,
    k_ref,
    v_ref,
    x_ref,
    g_ref,
    b_ref,
    c_ref,
    kvo,
    kvx,
    tx1,
    rx1,
    tx2,
    rx2,
    hkt,
    hkr,
    hst,
    hsr,
    log_ref,
    mt_ref,
    bt_ref,
    xw_ref,
    gm_ref,
    el_ref,
    sg_ref,
    qt_ref,
    sc_ref,
    wt_ref,
    top_ref,
    den_ref,
    acc_ref,
    state_ref,
    loads,
    s1,
    r1,
    s2,
    r2,
    up,
    down,
    ro,
    sx,
    rx,
    sk,
    rk,
    sf,
    rf,
):
    s, t, r = lax.axis_index("seq"), lax.axis_index("tp"), lax.axis_index("role")
    row = s // RING
    z = lax.rem(s, RING)
    across = (lax.rem(s + RING, SEQ), t, r)

    fetched = [
        pltpu.make_async_copy(src.at[0], dst, loads.at[i])
        for i, (src, dst) in enumerate(
            [
                (k_hbm, k_ref),
                (v_hbm, v_ref),
                (b_hbm, b_ref),
                (x_hbm, x_ref),
                (c_hbm, c_ref),
                (g_hbm, g_ref),
                (q_hbm, q_ref),
            ]
        )
    ]
    for copy in fetched:
        copy.start()

    def on_ring(step):
        return (row * RING + lax.rem(z + step + RING, RING), t, r)

    def owner_hop(level):
        if level == 0:
            return (s, t, 1 - r)
        width = 1 << (level - 1)
        return (s, t + width * (1 - 2 * lax.rem(t // width, 2)), r)

    def send(src, dst, ssem, rsem, device):
        return pltpu.make_async_remote_copy(
            src, dst, ssem, rsem, device_id=device, device_id_type=MESH
        )

    barrier = pltpu.get_barrier_semaphore()
    for k in range(1, SEQ):
        pl.semaphore_signal(
            barrier, inc=1, device_id=(lax.rem(s + k, SEQ), t, r), device_id_type=MESH
        )
    for level in range(4):
        pl.semaphore_signal(barrier, inc=1, device_id=owner_hop(level), device_id_type=MESH)

    def up_copy(slot):
        return send(kvo.at[slot], kvo.at[slot], up.at[slot], ro.at[slot], on_ring(1))

    def down_copy(slot):
        return send(kvo.at[slot], kvo.at[slot], down.at[slot], ro.at[slot], on_ring(-1))

    def cross_copy(slot):
        return send(kvo.at[slot], kvx.at[slot], sx.at[slot], rx.at[slot], across)

    def kv_hop(level):
        return send(
            hkt.at[level], hkr.at[level], sk.at[level], rk.at[level], owner_hop(level)
        )

    def state_hop(level):
        return send(
            hst.at[level], hsr.at[level], sf.at[level], rf.at[level], owner_hop(level)
        )

    def local_copy(pair):
        return send(tx1.at[pair], rx1.at[s], s1.at[pair], r1.at[s], (pair, t, r))

    def local_arrival(source):
        return send(tx1.at[source], rx1.at[source], s1.at[source], r1.at[source], (source, t, r))

    def prefix_copy(target):
        return send(tx2.at[target], rx2.at[s], s2.at[target], r2.at[s], (target, t, r))

    def prefix_arrival(pair):
        return send(tx2.at[pair], rx2.at[pair], s2.at[pair], r2.at[pair], (pair, t, r))

    length = len_ref[0]
    live = s * ROWS + iota((ROWS, LANES), 0) < length
    low = iota((ROWS, LANES), 1) < 64

    steps = jnp.concatenate(
        [st_ref[0].astype(F32), jnp.zeros((LANES - 32, ROWS), F32)], axis=0
    ).T
    rates = jnp.concatenate([rate_ref[...], jnp.zeros((1, LANES - 32), F32)], axis=1)
    steps = jnp.where(live, steps, 0.0)
    causal = iota((ROWS, ROWS), 0) >= iota((ROWS, ROWS), 1)
    logs = jnp.dot(
        causal.astype(F32),
        steps * rates * -LOG2E,
        precision=lax.Precision.HIGHEST,
        preferred_element_type=F32,
    )
    used = steps > 0.0
    less = jnp.where(used, logs - jnp.log(jnp.where(used, steps, 1.0)) * LOG2E, 1e9)
    log_ref[...] = logs
    weights = jnp.exp2(logs[ROWS - 1 :, :] - less)
    decays = jnp.exp2(logs[ROWS - 8 :, :])
    mt_ref[...] = less.T

    for copy in fetched[:2]:
        copy.wait()
    keys = jnp.where(live, k_ref[...].astype(F32), 0.0)
    values = jnp.where(live, v_ref[...].astype(F32), 0.0)
    flipped = values.T.astype(BF16)
    hkt[0, 0] = keys.astype(BF16)
    hkt[0, 1] = values.astype(BF16)
    kvo[z, 0] = keys.astype(BF16)
    kvo[z, 1, :LANES] = flipped[:, :LANES]
    kvo[z, 1, LANES:] = flipped[:, LANES:]
    pl.semaphore_wait(barrier, SEQ - 1 + 4)
    up_copy(z).start()
    down_copy(z).start()

    @pl.when(row == 0)
    def _():
        cross_copy(z).start()

    kv_hop(0).start()

    for copy in fetched[2:4]:
        copy.wait()
    bt_ref[...] = b_ref[...].astype(F32).T.astype(BF16)
    which = iota((16, LANES), 0)
    for pair in range(SEQ):
        cols = slice(pair * LANES, (pair + 1) * LANES)
        one, two = 2 * pair, 2 * pair + 1
        weight = jnp.where(low, weights[:, one : one + 1], weights[:, two : two + 1])
        xw_ref[:, cols] = (x_ref[:, cols].astype(F32) * weight).astype(BF16)
        decay = jnp.where(low[:1], decays[7:8, one : one + 1], decays[7:8, two : two + 1])
        high = decay.astype(BF16).astype(F32)
        middle = (decay - high).astype(BF16).astype(F32)
        rest = decay - high - middle
        tx1[pair, STATE:, :] = jnp.where(
            which == 0, high, jnp.where(which == 1, middle, jnp.where(which == 2, rest, 0.0))
        ).astype(BF16)
    for twice in range(RING):
        fresh = jnp.dot(
            bt_ref[...],
            xw_ref[:, twice * 2 * LANES : (twice + 1) * 2 * LANES],
            preferred_element_type=F32,
        ).astype(BF16)
        tx1[2 * twice, :STATE, :] = fresh[:, :LANES]
        tx1[2 * twice + 1, :STATE, :] = fresh[:, LANES:]
    for k in range(1, 5):
        local_copy(lax.rem(s + k, SEQ)).start()
    rx1[s] = tx1[s]

    fetched[4].wait()
    gm_ref[...] = jnp.where(
        causal,
        lax.dot_general(
            c_ref[...], b_ref[...], (((1,), (1,)), ((), ())), preferred_element_type=F32
        ),
        0.0,
    )
    for copy in fetched[5:]:
        copy.wait()
    key_xor = own_ref[0]
    skips = jnp.broadcast_to(
        jnp.concatenate([skip_ref[...], jnp.zeros((1, LANES - 32), F32)], axis=1), (8, LANES)
    )

    def within(four):
        shift = lax.rem(LANES - 8 * four, LANES)
        turned = pltpu.roll(log_ref[...], shift, axis=1)
        gains = pltpu.roll(skips, shift, axis=1)
        table = mt_ref[pl.ds(pl.multiple_of(8 * four, 8), 8), :]
        for j in range(4):
            cols = pl.ds(pl.multiple_of((4 * four + j) * LANES, LANES), LANES)
            heads = [2 * j, 2 * j + 1]
            columns = [jnp.broadcast_to(turned[:, i : i + 1], (ROWS, LANES)) for i in heads]
            lines = [table[i : i + 1, :] for i in heads]
            x = x_ref[:, cols].astype(F32)
            halves = [jnp.where(low, x, 0.0).astype(BF16), jnp.where(low, 0.0, x).astype(BF16)]

            def mix(head, below, right):
                rows, over = slice(below, below + 128), slice(right, right + 128)
                spread = columns[head][rows] - lines[head][:, over]
                return (gm_ref[rows, over] * jnp.exp2(spread)).astype(BF16)

            gain = jnp.where(
                low[:1], gains[:1, heads[0] : heads[0] + 1], gains[:1, heads[1] : heads[1] + 1]
            )
            skipped = gain * x
            upper = jnp.dot(
                jnp.concatenate([mix(0, 0, 0), mix(1, 0, 0)], axis=1),
                jnp.concatenate([halves[0][:128], halves[1][:128]], axis=0),
                preferred_element_type=F32,
            )
            lower = jnp.dot(
                jnp.concatenate(
                    [mix(0, 128, 0), mix(0, 128, 128), mix(1, 128, 0), mix(1, 128, 128)], axis=1
                ),
                jnp.concatenate(halves, axis=0),
                preferred_element_type=F32,
            )
            y_ref[:128, cols] = upper + skipped[:128]
            y_ref[128:, cols] = lower + skipped[128:]
            el_ref[:, cols] = jnp.exp2(jnp.where(low, columns[0], columns[1]))
            gate = g_ref[:, cols].astype(F32)
            sg_ref[:, cols] = gate / (1.0 + jnp.exp(-gate))

    def routed(level, arrived, held):
        bit = lax.rem(key_xor // (1 << (level - 1)), 2)
        take = jnp.broadcast_to(bit, arrived.shape) == 1
        return jnp.where(take, arrived.astype(F32), held.astype(F32)).astype(BF16)

    def kv_step(level):
        kv_hop(level).wait_recv()
        for part in range(2):
            moved = hkr[level, part]
            if level > 0:
                moved = routed(level, moved, hkt[level, part])
            if level < 3:
                hkt[level + 1, part] = moved
            else:
                dk_ref[0, part] = moved
        if level < 3:
            kv_hop(level + 1).start()

    def ring_turn(four, carry):
        within(four)
        for j in range(2):
            h = 2 * four + j
            cols = pl.ds(pl.multiple_of(h * LANES, LANES), LANES)
            qt_ref[h] = q_ref[:, cols].astype(F32).T.astype(BF16)
        before = lax.rem(z - four - 1 + RING, RING)
        after = lax.rem(z + four + 1, RING)
        up_copy(before).wait_recv()

        @pl.when(four < 3)
        def _():
            up_copy(before).start()
            down_copy(after).wait_recv()

        @pl.when(four < 2)
        def _():
            down_copy(after).start()

        @pl.when(four < 2)
        def _():
            for j in range(4):
                local_copy(lax.rem(s + 4 * four + 5 + j, SEQ)).start()

        @pl.when(four == 2)
        def _():
            for j in range(3):
                local_copy(lax.rem(s + 13 + j, SEQ)).start()

        @pl.when(row == 0)
        def _():
            cross_copy(before).start()

            @pl.when(four < 3)
            def _():
                cross_copy(after).start()

        for level in range(4):

            @pl.when(four == level)
            def _():
                kv_step(level)

        return carry

    lax.fori_loop(0, 4, ring_turn, 0)

    state_ref[...] = jnp.zeros((STATE, LANES), F32)

    def scan(i, carry):
        now = state_ref[...]
        tx2[i] = now.astype(BF16)

        @pl.when(i == s)
        def _():
            rx2[s] = now.astype(BF16)

        @pl.when(i != s)
        def _():
            prefix_copy(i).start()
            local_arrival(i).wait_recv()

        decay = jnp.sum(rx1[i, STATE:, :].astype(F32), axis=0, keepdims=True)
        state_ref[...] = now * decay + rx1[i, :STATE, :].astype(F32)
        return carry

    lax.fori_loop(0, SEQ, scan, 0)
    hst[0] = state_ref[...].astype(BF16)
    state_hop(0).start()

    def state_step(level):
        state_hop(level).wait_recv()
        moved = hsr[level]
        if level > 0:
            moved = routed(level, moved, hst[level])
        if level < 3:
            hst[level + 1] = moved
            state_hop(level + 1).start()
        else:
            ds_ref[0] = moved.astype(F32).T.reshape(2, 64, STATE)

    top_ref[...] = jnp.full(top_ref.shape, -1e30, F32)
    den_ref[...] = jnp.zeros(den_ref.shape, F32)
    acc_ref[...] = jnp.zeros(acc_ref.shape, F32)

    def attend(kv, first, ahead):
        def score(h):
            for w in range(4):
                sc_ref[h % 2, w * ROWS : (w + 1) * ROWS] = jnp.dot(
                    kv[first + w, 0], qt_ref[h], preferred_element_type=F32
                )

        def soften(h):
            scores = sc_ref[h % 2]
            if ahead is not None:
                apart = iota((4 * ROWS, ROWS), 0) - iota((4 * ROWS, ROWS), 1)
                scores = jnp.where(apart <= ahead, scores, -jnp.inf)
            old = top_ref[h]
            new = jnp.maximum(old, jnp.max(scores, axis=0, keepdims=True) * SCORE)
            weight = jnp.exp2(scores * SCORE - new)
            scale = jnp.exp2(old - new)
            wt_ref[h % 2] = weight.astype(BF16)
            den_ref[h] = den_ref[h] * scale + jnp.sum(weight, axis=0, keepdims=True)
            top_ref[h] = new
            return scale

        def mix(h, scale):
            part = 0.0
            for w in range(4):
                flat = kv[first + w, 1]
                part = part + jnp.dot(
                    jnp.concatenate([flat[:LANES], flat[LANES:]], axis=1),
                    wt_ref[h % 2, w * ROWS : (w + 1) * ROWS],
                    preferred_element_type=F32,
                )
            acc_ref[h] = acc_ref[h] * scale + part

        score(0)
        for h in range(HEADS):
            if h + 1 < HEADS:
                score(h + 1)
            mix(h, soften(h))

    def own_row(part, carry):
        @pl.when(z >= 4 * part)
        def _():
            attend(kvo, 4 * part, z * ROWS - part * 4 * ROWS)

        for level in range(2):

            @pl.when(part == level)
            def _():
                state_step(level)

        return carry

    lax.fori_loop(0, 2, own_row, 0)

    def other_row(part, carry):
        @pl.when(row == 1)
        def _():
            for w in range(4):
                cross_copy(4 * part + w).wait_recv()
            attend(kvx, 4 * part, None)

        for level in range(2):

            @pl.when(part == level)
            def _():
                state_step(level + 2)

        return carry

    lax.fori_loop(0, 2, other_row, 0)

    for h in range(HEADS):
        attended = (acc_ref[h] / den_ref[h]).T
        ao_ref[0, :, h * LANES : (h + 1) * LANES] = jnp.where(live, attended, 0.0).astype(BF16)

    sq_ref[...] = jnp.zeros((ROWS, LANES), F32)

    def outputs(twice, carry):
        pairs = [lax.rem(s + 2 * twice + j, SEQ) for j in range(2)]
        for j, pair in enumerate(pairs):
            if j == 0:

                @pl.when(twice > 0)
                def _():
                    prefix_arrival(pair).wait_recv()

            else:
                prefix_arrival(pair).wait_recv()
        carried = jnp.dot(
            c_ref[...],
            jnp.concatenate([rx2[pair] for pair in pairs], axis=1),
            preferred_element_type=F32,
        )
        for j, pair in enumerate(pairs):
            cols = pl.ds(pl.multiple_of(pair * LANES, LANES), LANES)
            mine = carried[:, j * LANES : (j + 1) * LANES]
            mixed = (y_ref[:, cols] + el_ref[:, cols] * mine).astype(BF16).astype(F32)
            gated = mixed * sg_ref[:, cols]
            y_ref[:, cols] = gated
            sq_ref[...] += gated * gated
        return carry

    lax.fori_loop(0, RING, outputs, 0)
    mean = jnp.sum(sq_ref[...], axis=1, keepdims=True) * (1.0 / 2048.0)
    sq_ref[...] = jnp.where(live, lax.rsqrt(mean + 1e-05), 0.0)

    for k in range(1, SEQ):
        local_copy(lax.rem(s + k, SEQ)).wait_send()
        prefix_copy(lax.rem(s + k, SEQ)).wait_send()
    for k in range(4):
        up_copy(lax.rem(z - k + RING, RING)).wait_send()
    for k in range(3):
        down_copy(lax.rem(z + k, RING)).wait_send()

    @pl.when(row == 0)
    def _():
        for slot in range(RING):
            cross_copy(slot).wait_send()

    for level in range(4):
        kv_hop(level).wait_send()
        state_hop(level).wait_send()


def finish(y_ref, factor_ref, gain_ref, ao_in, ds_in, dk_in, mo_ref, ao_ref, ds_ref, dk_ref):
    for i in range(y_ref.shape[1] // LANES):
        cols = slice(i * LANES, (i + 1) * LANES)
        mo_ref[0, :, cols] = (y_ref[:, cols] * factor_ref[...] * gain_ref[:, cols]).astype(BF16)
    ao_ref[...] = ao_in[...]
    ds_ref[...] = ds_in[...]
    dk_ref[...] = dk_in[...]


def on_device(
    prompt_length,
    owner_map,
    queries,
    key_rows,
    value_matrix,
    ssm_input,
    gate_input,
    step_sizes,
    decay_rate,
    skip_gain,
    write_proj,
    read_proj,
    norm_gain,
):
    smem = pl.BlockSpec(memory_space=pltpu.SMEM)
    vmem = pl.BlockSpec(memory_space=pltpu.VMEM)
    hbm = pl.BlockSpec(memory_space=pltpu.HBM)
    dma = pltpu.SemaphoreType.DMA
    wide = pltpu.VMEM((ROWS, SEQ * LANES), F32)
    tokens = pltpu.VMEM((ROWS, SEQ * LANES), BF16)
    square = pltpu.VMEM((ROWS, LANES), F32)
    narrow = pltpu.VMEM((ROWS, LANES), BF16)
    group = pltpu.VMEM((ROWS, STATE), BF16)
    block = pltpu.VMEM((RING, 2, ROWS, LANES), BF16)
    gated, factor, attn, state, kv = pl.pallas_call(
        kernel,
        name="prefill",
        out_shape=(
            jax.ShapeDtypeStruct((ROWS, 2048), F32),
            jax.ShapeDtypeStruct((ROWS, LANES), F32),
            jax.ShapeDtypeStruct((1, ROWS, 1024), BF16),
            jax.ShapeDtypeStruct((1, 2, 64, STATE), F32),
            jax.ShapeDtypeStruct((1, 2, ROWS, LANES), BF16),
        ),
        in_specs=[smem, smem, hbm, hbm, hbm, hbm, hbm, vmem, vmem, vmem, hbm, hbm],
        out_specs=(vmem,) * 5,
        scratch_shapes=[
            pltpu.VMEM((ROWS, 1024), BF16),
            narrow,
            narrow,
            tokens,
            tokens,
            group,
            group,
            block,
            block,
            pltpu.VMEM((SEQ, MSG, LANES), BF16),
            pltpu.VMEM((SEQ, MSG, LANES), BF16),
            pltpu.VMEM((SEQ, STATE, LANES), BF16),
            pltpu.VMEM((SEQ, STATE, LANES), BF16),
            pltpu.VMEM((4, 2, ROWS, LANES), BF16),
            pltpu.VMEM((4, 2, ROWS, LANES), BF16),
            pltpu.VMEM((4, STATE, LANES), BF16),
            pltpu.VMEM((4, STATE, LANES), BF16),
            square,
            pltpu.VMEM((LANES, ROWS), F32),
            group,
            tokens,
            pltpu.VMEM((ROWS, ROWS), F32),
            wide,
            wide,
            pltpu.VMEM((HEADS, LANES, ROWS), BF16),
            pltpu.VMEM((2, 4 * ROWS, ROWS), F32),
            pltpu.VMEM((2, 4 * ROWS, ROWS), BF16),
            pltpu.VMEM((HEADS, 1, ROWS), F32),
            pltpu.VMEM((HEADS, 1, ROWS), F32),
            pltpu.VMEM((HEADS, LANES, ROWS), F32),
            pltpu.VMEM((STATE, LANES), F32),
            dma((7,)),
            dma((SEQ,)),
            dma((SEQ,)),
            dma((SEQ,)),
            dma((SEQ,)),
            dma((RING,)),
            dma((RING,)),
            dma((RING,)),
            dma((RING,)),
            dma((RING,)),
            dma((4,)),
            dma((4,)),
            dma((4,)),
            dma((4,)),
        ],
        compiler_params=pltpu.CompilerParams(
            collective_id=0, has_side_effects=True, vmem_limit_bytes=63 * 2**20
        ),
    )(
        prompt_length,
        owner_map,
        queries,
        key_rows,
        value_matrix,
        ssm_input,
        gate_input,
        jnp.swapaxes(step_sizes, 1, 2),
        decay_rate.reshape(1, 32),
        skip_gain.reshape(1, 32),
        write_proj,
        read_proj,
    )
    part = 512
    passed = [
        pl.BlockSpec((1, ROWS, 256), lambda i: (0, 0, i)),
        pl.BlockSpec((1, 2, 16, STATE), lambda i: (0, 0, i, 0)),
        pl.BlockSpec((1, 2, 64, LANES), lambda i: (0, 0, i, 0)),
    ]
    return pl.pallas_call(
        finish,
        name="finish",
        grid=(2048 // part,),
        out_shape=(
            jax.ShapeDtypeStruct((1, ROWS, 2048), BF16),
            jax.ShapeDtypeStruct(attn.shape, attn.dtype),
            jax.ShapeDtypeStruct(state.shape, state.dtype),
            jax.ShapeDtypeStruct(kv.shape, kv.dtype),
        ),
        in_specs=[
            pl.BlockSpec((ROWS, part), lambda i: (0, i)),
            pl.BlockSpec((ROWS, LANES), lambda i: (0, 0)),
            pl.BlockSpec((1, part), lambda i: (0, i)),
            *passed,
        ],
        out_specs=(pl.BlockSpec((1, ROWS, part), lambda i: (0, 0, i)), *passed),
    )(gated, factor, norm_gain.reshape(1, 2048), attn, state, kv)


def solution(mesh):
    tokens = P("role", "seq", "tp")
    in_specs = (
        P("role"),
        P(),
        tokens,
        tokens,
        tokens,
        tokens,
        tokens,
        tokens,
        P("tp"),
        P("tp"),
        tokens,
        tokens,
        P("tp"),
    )
    out_specs = (
        tokens,
        tokens,
        P("role", ("tp", "seq"), None, None),
        P("role", None, "seq", "tp"),
    )
    return jax.shard_map(
        on_device, mesh=mesh, in_specs=in_specs, out_specs=out_specs, check_vma=False
    )
```

time: 100 us -> 84.3 us (0.84)
  the two profiles are of different devices: /device:TPU:230 before, /device:TPU:6 now
where the time goes in v2:
time: 84.3 us; the launch traced here: 83.8 us
  Pallas kernels  82.5 us (98%)
  between operations  1.29 us (2%)
    pallas_call x1, Pallas kernels, on_device(): pl.pallas_call(kernel, name='prefill', out_shape=(jax.ShapeDtypeStruct((R...  78.5 us
    pallas_call x1, Pallas kernels, on_device(): pl.pallas_call(finish, name='finish', grid=(2048 // part,), out_shape=(ja...  3.96 us

profile of v2, /device:TPU:6, one launch (start us, length us, event | category | flops | bytes accessed | tf_op | source)
XLA Modules:
  0.0 83.8 jit_solution(15916078744757268921)
XLA Ops:
  1.3 78.5 %prefill.1 = (f32[256,2048]{1,0:T(8,128)}, f32[256,128]{1,0:T(8,128)}, bf16[1,256,1024]{2,1,0:T(8,128)(2,1)}, f32[1,2,64,256]{3,2,1,0:T(8,128)}, bf16[1,2,256,128]{3,2,1,0:T(8,128)(2,1)}) custom-call(s32[1]{0:T(128)S(6)} %copy.17.len_ref, s32[8]{0:T(128)} %own_ref.1, bf16[1,256,1024]{2,1,0:T(8,128)(2,1)} %q_hbm.1, bf16[1,256,128]{2,1,0:T(8,128)(2,1)} %k_hbm.1, ...), custom_call_target="tpu_custom_call" | custom-call | tf_op jit(solution)/shard_map/prefill/pallas_call | solution.py:551
  79.8 4.0 %finish.1 = (bf16[1,256,2048]{2,1,0:T(8,128)(2,1)}, bf16[1,256,1024]{2,1,0:T(8,128)(2,1)}, f32[1,2,64,256]{3,2,1,0:T(8,128)}, bf16[1,2,256,128]{3,2,1,0:T(8,128)(2,1)}) custom-call(f32[256,2048]{1,0:T(8,128)} %get-tuple-element.9.y_ref, f32[256,128]{1,0:T(8,128)} %get-tuple-element.10.factor_ref, f32[1,2048]{1,0:T(1,128)} %bitcast.5, ...), custom_call_target="tpu_custom_call" | custom-call | tf_op jit(solution)/shard_map/finish/pallas_call | solution.py:633

commit v3 on v2

--- a/solution.py
+++ b/solution.py
@@ -14,7 +14,8 @@
 RING = 8
 HEADS = 8
 STATE = 256
-MSG = STATE + 16
+HEAD = 16
+HALF = STATE // 2
 F32 = jnp.float32
 BF16 = jnp.bfloat16
 
@@ -150,17 +151,40 @@
             hst.at[level], hsr.at[level], sf.at[level], rf.at[level], owner_hop(level)
         )
 
-    def local_copy(pair):
-        return send(tx1.at[pair], rx1.at[s], s1.at[pair], r1.at[s], (pair, t, r))
-
-    def local_arrival(source):
-        return send(tx1.at[source], rx1.at[source], s1.at[source], r1.at[source], (source, t, r))
-
-    def prefix_copy(target):
-        return send(tx2.at[target], rx2.at[s], s2.at[target], r2.at[s], (target, t, r))
-
-    def prefix_arrival(pair):
-        return send(tx2.at[pair], rx2.at[pair], s2.at[pair], r2.at[pair], (pair, t, r))
+    def part_rows(part, first):
+        return pl.ds(first + part * HALF, HALF) if part else pl.ds(0, first + HALF)
+
+    def local_send(here, there, part, device):
+        rows = part_rows(part, HEAD)
+        return send(
+            tx1.at[here, rows],
+            rx1.at[there, rows],
+            s1.at[part * SEQ + here],
+            r1.at[part * SEQ + there],
+            (device, t, r),
+        )
+
+    def prefix_send(here, there, part, device):
+        rows = part_rows(part, 0)
+        return send(
+            tx2.at[here, rows],
+            rx2.at[there, rows],
+            s2.at[part * SEQ + here],
+            r2.at[part * SEQ + there],
+            (device, t, r),
+        )
+
+    def local_copy(pair, part):
+        return local_send(pair, s, part, pair)
+
+    def local_arrival(source, part):
+        return local_send(source, source, part, source)
+
+    def prefix_copy(target, part):
+        return prefix_send(target, s, part, target)
+
+    def prefix_arrival(pair, part):
+        return prefix_send(pair, pair, part, pair)
 
     length = len_ref[0]
     live = s * ROWS + iota((ROWS, LANES), 0) < length
@@ -218,7 +242,7 @@
         high = decay.astype(BF16).astype(F32)
         middle = (decay - high).astype(BF16).astype(F32)
         rest = decay - high - middle
-        tx1[pair, STATE:, :] = jnp.where(
+        tx1[pair, :HEAD, :] = jnp.where(
             which == 0, high, jnp.where(which == 1, middle, jnp.where(which == 2, rest, 0.0))
         ).astype(BF16)
     for twice in range(RING):
@@ -227,10 +251,16 @@
             xw_ref[:, twice * 2 * LANES : (twice + 1) * 2 * LANES],
             preferred_element_type=F32,
         ).astype(BF16)
-        tx1[2 * twice, :STATE, :] = fresh[:, :LANES]
-        tx1[2 * twice + 1, :STATE, :] = fresh[:, LANES:]
-    for k in range(1, 5):
-        local_copy(lax.rem(s + k, SEQ)).start()
+        tx1[2 * twice, HEAD:, :] = fresh[:, :LANES]
+        tx1[2 * twice + 1, HEAD:, :] = fresh[:, LANES:]
+    groups = [(0, 1, 9), (0, 9, SEQ), (1, 1, 9), (1, 9, SEQ)]
+
+    def send_group(index):
+        part, first, end = groups[index]
+        for k in range(first, end):
+            local_copy(lax.rem(s + k, SEQ), part).start()
+
+    send_group(0)
     rx1[s] = tx1[s]
 
     fetched[4].wait()
@@ -325,15 +355,11 @@
         def _():
             down_copy(after).start()
 
-        @pl.when(four < 2)
-        def _():
-            for j in range(4):
-                local_copy(lax.rem(s + 4 * four + 5 + j, SEQ)).start()
-
-        @pl.when(four == 2)
-        def _():
-            for j in range(3):
-                local_copy(lax.rem(s + 13 + j, SEQ)).start()
+        for index in range(1, 4):
+
+            @pl.when(four == index - 1)
+            def _():
+                send_group(index)
 
         @pl.when(row == 0)
         def _():
@@ -355,24 +381,31 @@
 
     state_ref[...] = jnp.zeros((STATE, LANES), F32)
 
-    def scan(i, carry):
-        now = state_ref[...]
-        tx2[i] = now.astype(BF16)
-
-        @pl.when(i == s)
-        def _():
-            rx2[s] = now.astype(BF16)
-
-        @pl.when(i != s)
-        def _():
-            prefix_copy(i).start()
-            local_arrival(i).wait_recv()
-
-        decay = jnp.sum(rx1[i, STATE:, :].astype(F32), axis=0, keepdims=True)
-        state_ref[...] = now * decay + rx1[i, :STATE, :].astype(F32)
-        return carry
-
-    lax.fori_loop(0, SEQ, scan, 0)
+    def scan(part):
+        rows = slice(part * HALF, (part + 1) * HALF)
+        stored = slice(HEAD + part * HALF, HEAD + (part + 1) * HALF)
+
+        def turn(i, carry):
+            now = state_ref[rows]
+            tx2[i, rows] = now.astype(BF16)
+
+            @pl.when(i == s)
+            def _():
+                rx2[s, rows] = now.astype(BF16)
+
+            @pl.when(i != s)
+            def _():
+                prefix_copy(i, part).start()
+                local_arrival(i, part).wait_recv()
+
+            decay = jnp.sum(rx1[i, :HEAD, :].astype(F32), axis=0, keepdims=True)
+            state_ref[rows] = now * decay + rx1[i, stored, :].astype(F32)
+            return carry
+
+        lax.fori_loop(0, SEQ, turn, 0)
+
+    scan(0)
+    scan(1)
     hst[0] = state_ref[...].astype(BF16)
     state_hop(0).start()
 
@@ -467,38 +500,45 @@
 
     sq_ref[...] = jnp.zeros((ROWS, LANES), F32)
 
-    def outputs(twice, carry):
-        pairs = [lax.rem(s + 2 * twice + j, SEQ) for j in range(2)]
-        for j, pair in enumerate(pairs):
-            if j == 0:
-
-                @pl.when(twice > 0)
-                def _():
-                    prefix_arrival(pair).wait_recv()
-
-            else:
-                prefix_arrival(pair).wait_recv()
-        carried = jnp.dot(
-            c_ref[...],
-            jnp.concatenate([rx2[pair] for pair in pairs], axis=1),
-            preferred_element_type=F32,
-        )
-        for j, pair in enumerate(pairs):
-            cols = pl.ds(pl.multiple_of(pair * LANES, LANES), LANES)
-            mine = carried[:, j * LANES : (j + 1) * LANES]
-            mixed = (y_ref[:, cols] + el_ref[:, cols] * mine).astype(BF16).astype(F32)
-            gated = mixed * sg_ref[:, cols]
-            y_ref[:, cols] = gated
-            sq_ref[...] += gated * gated
-        return carry
-
-    lax.fori_loop(0, RING, outputs, 0)
+    def outputs(part):
+        rows = slice(part * HALF, (part + 1) * HALF)
+
+        def turn(twice, carry):
+            pairs = [lax.rem(s + 2 * twice + j, SEQ) for j in range(2)]
+
+            @pl.when(twice > 0)
+            def _():
+                prefix_arrival(pairs[0], part).wait_recv()
+
+            prefix_arrival(pairs[1], part).wait_recv()
+            carried = jnp.dot(
+                c_ref[:, rows],
+                jnp.concatenate([rx2[pair, rows] for pair in pairs], axis=1),
+                preferred_element_type=F32,
+            )
+            for j, pair in enumerate(pairs):
+                cols = pl.ds(pl.multiple_of(pair * LANES, LANES), LANES)
+                mine = carried[:, j * LANES : (j + 1) * LANES]
+                total = y_ref[:, cols] + el_ref[:, cols] * mine
+                if part == 0:
+                    y_ref[:, cols] = total
+                else:
+                    gated = total.astype(BF16).astype(F32) * sg_ref[:, cols]
+                    y_ref[:, cols] = gated
+                    sq_ref[...] += gated * gated
+            return carry
+
+        lax.fori_loop(0, RING, turn, 0)
+
+    outputs(0)
+    outputs(1)
     mean = jnp.sum(sq_ref[...], axis=1, keepdims=True) * (1.0 / 2048.0)
     sq_ref[...] = jnp.where(live, lax.rsqrt(mean + 1e-05), 0.0)
 
     for k in range(1, SEQ):
-        local_copy(lax.rem(s + k, SEQ)).wait_send()
-        prefix_copy(lax.rem(s + k, SEQ)).wait_send()
+        for part in range(2):
+            local_copy(lax.rem(s + k, SEQ), part).wait_send()
+            prefix_copy(lax.rem(s + k, SEQ), part).wait_send()
     for k in range(4):
         up_copy(lax.rem(z - k + RING, RING)).wait_send()
     for k in range(3):
@@ -570,8 +610,8 @@
             group,
             block,
             block,
-            pltpu.VMEM((SEQ, MSG, LANES), BF16),
-            pltpu.VMEM((SEQ, MSG, LANES), BF16),
+            pltpu.VMEM((SEQ, HEAD + STATE, LANES), BF16),
+            pltpu.VMEM((SEQ, HEAD + STATE, LANES), BF16),
             pltpu.VMEM((SEQ, STATE, LANES), BF16),
             pltpu.VMEM((SEQ, STATE, LANES), BF16),
             pltpu.VMEM((4, 2, ROWS, LANES), BF16),
@@ -593,10 +633,10 @@
             pltpu.VMEM((HEADS, LANES, ROWS), F32),
             pltpu.VMEM((STATE, LANES), F32),
             dma((7,)),
-            dma((SEQ,)),
-            dma((SEQ,)),
-            dma((SEQ,)),
-            dma((SEQ,)),
+            dma((2 * SEQ,)),
+            dma((2 * SEQ,)),
+            dma((2 * SEQ,)),
+            dma((2 * SEQ,)),
             dma((RING,)),
             dma((RING,)),
             dma((RING,)),
@@ -624,11 +664,11 @@
         write_proj,
         read_proj,
     )
-    part = 512
+    part = 1024
     passed = [
-        pl.BlockSpec((1, ROWS, 256), lambda i: (0, 0, i)),
-        pl.BlockSpec((1, 2, 16, STATE), lambda i: (0, 0, i, 0)),
-        pl.BlockSpec((1, 2, 64, LANES), lambda i: (0, 0, i, 0)),
+        pl.BlockSpec((1, ROWS, 512), lambda i: (0, 0, i)),
+        pl.BlockSpec((1, 2, 32, STATE), lambda i: (0, 0, i, 0)),
+        pl.BlockSpec((1, 2, 128, LANES), lambda i: (0, 0, i, 0)),
     ]
     return pl.pallas_call(
         finish,

time: 84.3 us -> 79.5 us (0.943)
  the two profiles are of different devices: /device:TPU:6 before, /device:TPU:32 now
where the time goes in v3:
time: 79.5 us; the launch traced here: 79.3 us
  Pallas kernels  78 us (98%)
  between operations  1.29 us (2%)
    pallas_call x1, Pallas kernels, on_device(): pl.pallas_call(kernel, name='prefill', out_shape=(jax.ShapeDtypeStruct((R...  75.1 us
    pallas_call x1, Pallas kernels, on_device(): pl.pallas_call(finish, name='finish', grid=(2048 // part,), out_shape=(ja...  2.85 us

profile of v3, /device:TPU:32, one launch (start us, length us, event | category | flops | bytes accessed | tf_op | source)
XLA Modules:
  0.0 79.3 jit_solution(3903296538259554785)
XLA Ops:
  1.3 75.1 %prefill.1 = (f32[256,2048]{1,0:T(8,128)}, f32[256,128]{1,0:T(8,128)}, bf16[1,256,1024]{2,1,0:T(8,128)(2,1)}, f32[1,2,64,256]{3,2,1,0:T(8,128)}, bf16[1,2,256,128]{3,2,1,0:T(8,128)(2,1)}) custom-call(s32[1]{0:T(128)S(6)} %copy.17.len_ref, s32[8]{0:T(128)} %own_ref.1, bf16[1,256,1024]{2,1,0:T(8,128)(2,1)} %q_hbm.1, bf16[1,256,128]{2,1,0:T(8,128)(2,1)} %k_hbm.1, ...), custom_call_target="tpu_custom_call" | custom-call | tf_op jit(solution)/shard_map/prefill/pallas_call | solution.py:591
  76.4 2.9 %finish.1 = (bf16[1,256,2048]{2,1,0:T(8,128)(2,1)}, bf16[1,256,1024]{2,1,0:T(8,128)(2,1)}, f32[1,2,64,256]{3,2,1,0:T(8,128)}, bf16[1,2,256,128]{3,2,1,0:T(8,128)(2,1)}) custom-call(f32[256,2048]{1,0:T(8,128)} %get-tuple-element.9.y_ref, f32[256,128]{1,0:T(8,128)} %get-tuple-element.10.factor_ref, f32[1,2048]{1,0:T(1,128)} %bitcast.5, ...), custom_call_target="tpu_custom_call" | custom-call | tf_op jit(solution)/shard_map/finish/pallas_call | solution.py:673

commit v4 on v3

--- a/solution.py
+++ b/solution.py
@@ -467,11 +467,9 @@
         def _():
             attend(kvo, 4 * part, z * ROWS - part * 4 * ROWS)
 
-        for level in range(2):
-
-            @pl.when(part == level)
-            def _():
-                state_step(level)
+        @pl.when(part == 1)
+        def _():
+            state_step(0)
 
         return carry
 
@@ -484,11 +482,9 @@
                 cross_copy(4 * part + w).wait_recv()
             attend(kvx, 4 * part, None)
 
-        for level in range(2):
-
-            @pl.when(part == level)
-            def _():
-                state_step(level + 2)
+        @pl.when(part == 1)
+        def _():
+            state_step(1)
 
         return carry
 
@@ -531,7 +527,9 @@
         lax.fori_loop(0, RING, turn, 0)
 
     outputs(0)
+    state_step(2)
     outputs(1)
+    state_step(3)
     mean = jnp.sum(sq_ref[...], axis=1, keepdims=True) * (1.0 / 2048.0)
     sq_ref[...] = jnp.where(live, lax.rsqrt(mean + 1e-05), 0.0)
 

time: 79.5 us -> 78.2 us (0.984)
  the two profiles are of different devices: /device:TPU:32 before, /device:TPU:6 now
where the time goes in v4:
time: 78.2 us; the launch traced here: 77.2 us
  Pallas kernels  75.9 us (97%)
  between operations  1.29 us (2%)
    pallas_call x1, Pallas kernels, on_device(): pl.pallas_call(kernel, name='prefill', out_shape=(jax.ShapeDtypeStruct((R...  73.1 us
    pallas_call x1, Pallas kernels, on_device(): pl.pallas_call(finish, name='finish', grid=(2048 // part,), out_shape=(ja...  2.85 us

profile of v4, /device:TPU:6, one launch (start us, length us, event | category | flops | bytes accessed | tf_op | source)
XLA Modules:
  0.0 77.2 jit_solution(8517243570148733402)
XLA Ops:
  1.3 73.1 %prefill.1 = (f32[256,2048]{1,0:T(8,128)}, f32[256,128]{1,0:T(8,128)}, bf16[1,256,1024]{2,1,0:T(8,128)(2,1)}, f32[1,2,64,256]{3,2,1,0:T(8,128)}, bf16[1,2,256,128]{3,2,1,0:T(8,128)(2,1)}) custom-call(s32[1]{0:T(128)S(6)} %copy.17.len_ref, s32[8]{0:T(128)} %own_ref.1, bf16[1,256,1024]{2,1,0:T(8,128)(2,1)} %q_hbm.1, bf16[1,256,128]{2,1,0:T(8,128)(2,1)} %k_hbm.1, ...), custom_call_target="tpu_custom_call" | custom-call | tf_op jit(solution)/shard_map/prefill/pallas_call | solution.py:589
  74.4 2.9 %finish.1 = (bf16[1,256,2048]{2,1,0:T(8,128)(2,1)}, bf16[1,256,1024]{2,1,0:T(8,128)(2,1)}, f32[1,2,64,256]{3,2,1,0:T(8,128)}, bf16[1,2,256,128]{3,2,1,0:T(8,128)(2,1)}) custom-call(f32[256,2048]{1,0:T(8,128)} %get-tuple-element.9.y_ref, f32[256,128]{1,0:T(8,128)} %get-tuple-element.10.factor_ref, f32[1,2048]{1,0:T(1,128)} %bitcast.5, ...), custom_call_target="tpu_custom_call" | custom-call | tf_op jit(solution)/shard_map/finish/pallas_call | solution.py:671

commit v5 on v4

--- a/solution.py
+++ b/solution.py
@@ -107,7 +107,7 @@
             ]
         )
     ]
-    for copy in fetched:
+    for copy in fetched[:4]:
         copy.start()
 
     def on_ring(step):
@@ -219,18 +219,10 @@
     kvo[z, 0] = keys.astype(BF16)
     kvo[z, 1, :LANES] = flipped[:, :LANES]
     kvo[z, 1, LANES:] = flipped[:, LANES:]
-    pl.semaphore_wait(barrier, SEQ - 1 + 4)
-    up_copy(z).start()
-    down_copy(z).start()
-
-    @pl.when(row == 0)
-    def _():
-        cross_copy(z).start()
-
-    kv_hop(0).start()
-
     for copy in fetched[2:4]:
         copy.wait()
+    for copy in fetched[4:]:
+        copy.start()
     bt_ref[...] = b_ref[...].astype(F32).T.astype(BF16)
     which = iota((16, LANES), 0)
     for pair in range(SEQ):
@@ -253,6 +245,16 @@
         ).astype(BF16)
         tx1[2 * twice, HEAD:, :] = fresh[:, :LANES]
         tx1[2 * twice + 1, HEAD:, :] = fresh[:, LANES:]
+    pl.semaphore_wait(barrier, SEQ - 1 + 4)
+    up_copy(z).start()
+    down_copy(z).start()
+
+    @pl.when(row == 0)
+    def _():
+        cross_copy(z).start()
+
+    kv_hop(0).start()
+
     groups = [(0, 1, 9), (0, 9, SEQ), (1, 1, 9), (1, 9, SEQ)]
 
     def send_group(index):
@@ -336,12 +338,41 @@
         if level < 3:
             kv_hop(level + 1).start()
 
+    state_ref[...] = jnp.zeros((STATE, LANES), F32)
+
+    def scan(part):
+        rows = slice(part * HALF, (part + 1) * HALF)
+        stored = slice(HEAD + part * HALF, HEAD + (part + 1) * HALF)
+
+        def turn(i, carry):
+            now = state_ref[rows]
+            tx2[i, rows] = now.astype(BF16)
+
+            @pl.when(i == s)
+            def _():
+                rx2[s, rows] = now.astype(BF16)
+
+            @pl.when(i != s)
+            def _():
+                prefix_copy(i, part).start()
+                local_arrival(i, part).wait_recv()
+
+            decay = jnp.sum(rx1[i, :HEAD, :].astype(F32), axis=0, keepdims=True)
+            state_ref[rows] = now * decay + rx1[i, stored, :].astype(F32)
+            return carry
+
+        lax.fori_loop(0, SEQ, turn, 0)
+
     def ring_turn(four, carry):
         within(four)
         for j in range(2):
             h = 2 * four + j
             cols = pl.ds(pl.multiple_of(h * LANES, LANES), LANES)
             qt_ref[h] = q_ref[:, cols].astype(F32).T.astype(BF16)
+        @pl.when(four == 3)
+        def _():
+            scan(0)
+
         before = lax.rem(z - four - 1 + RING, RING)
         after = lax.rem(z + four + 1, RING)
         up_copy(before).wait_recv()
@@ -379,32 +410,6 @@
 
     lax.fori_loop(0, 4, ring_turn, 0)
 
-    state_ref[...] = jnp.zeros((STATE, LANES), F32)
-
-    def scan(part):
-        rows = slice(part * HALF, (part + 1) * HALF)
-        stored = slice(HEAD + part * HALF, HEAD + (part + 1) * HALF)
-
-        def turn(i, carry):
-            now = state_ref[rows]
-            tx2[i, rows] = now.astype(BF16)
-
-            @pl.when(i == s)
-            def _():
-                rx2[s, rows] = now.astype(BF16)
-
-            @pl.when(i != s)
-            def _():
-                prefix_copy(i, part).start()
-                local_arrival(i, part).wait_recv()
-
-            decay = jnp.sum(rx1[i, :HEAD, :].astype(F32), axis=0, keepdims=True)
-            state_ref[rows] = now * decay + rx1[i, stored, :].astype(F32)
-            return carry
-
-        lax.fori_loop(0, SEQ, turn, 0)
-
-    scan(0)
     scan(1)
     hst[0] = state_ref[...].astype(BF16)
     state_hop(0).start()

time: 78.2 us -> 78 us (level)
  the two profiles are of different devices: /device:TPU:6 before, /device:TPU:196 now
where the time goes in v5:
time: 78 us; the launch traced here: 77.8 us
  Pallas kernels  76.5 us (98%)
  between operations  1.29 us (2%)
    pallas_call x1, Pallas kernels, on_device(): pl.pallas_call(kernel, name='prefill', out_shape=(jax.ShapeDtypeStruct((R...  73.7 us
    pallas_call x1, Pallas kernels, on_device(): pl.pallas_call(finish, name='finish', grid=(2048 // part,), out_shape=(ja...  2.85 us

profile of v5, /device:TPU:196, one launch (start us, length us, event | category | flops | bytes accessed | tf_op | source)
XLA Modules:
  0.0 77.8 jit_solution(1552101799988713581)
XLA Ops:
  1.3 73.7 %prefill.1 = (f32[256,2048]{1,0:T(8,128)}, f32[256,128]{1,0:T(8,128)}, bf16[1,256,1024]{2,1,0:T(8,128)(2,1)}, f32[1,2,64,256]{3,2,1,0:T(8,128)}, bf16[1,2,256,128]{3,2,1,0:T(8,128)(2,1)}) custom-call(s32[1]{0:T(128)S(6)} %copy.17.len_ref, s32[8]{0:T(128)} %own_ref.1, bf16[1,256,1024]{2,1,0:T(8,128)(2,1)} %q_hbm.1, bf16[1,256,128]{2,1,0:T(8,128)(2,1)} %k_hbm.1, ...), custom_call_target="tpu_custom_call" | custom-call | tf_op jit(solution)/shard_map/prefill/pallas_call | solution.py:594
  75.0 2.9 %finish.1 = (bf16[1,256,2048]{2,1,0:T(8,128)(2,1)}, bf16[1,256,1024]{2,1,0:T(8,128)(2,1)}, f32[1,2,64,256]{3,2,1,0:T(8,128)}, bf16[1,2,256,128]{3,2,1,0:T(8,128)(2,1)}) custom-call(f32[256,2048]{1,0:T(8,128)} %get-tuple-element.9.y_ref, f32[256,128]{1,0:T(8,128)} %get-tuple-element.10.factor_ref, f32[1,2048]{1,0:T(1,128)} %bitcast.5, ...), custom_call_target="tpu_custom_call" | custom-call | tf_op jit(solution)/shard_map/finish/pallas_call | solution.py:676
